TPU v7x, 32 devices: a whole 2x2x4 slice. The times are simulated.
32 devices in a mesh: lat: 4 (over y, x), lon: 8 (over z, core).
Axes of the slice: x: 2, y: 2, z: 4, core: 2. Of those that a mesh axis runs over, the one named last changes fastest.
Arguments:
- background: bfloat16 [4, 8, 512, 1024], P('lat', 'lon'), may hold values from -6 to 6
- conv_pert: bfloat16 [4, 8, 128, 512], P('lat', 'lon'), may hold values from -6 to 6
- conv_misfit: bfloat16 [4, 8, 128], P('lat', 'lon'), may hold values from -6 to 6
- conv_column: int32 [4, 8, 128], P('lat', 'lon'), may hold values from 0 to 255
- sat_pert: bfloat16 [4, 128, 32, 512], P('lat', 'lon'), may hold values from -6 to 6
- sat_misfit: bfloat16 [4, 128, 32], P('lat', 'lon'), may hold values from -6 to 6
- sat_rows: int32 [4, 128], P('lat', 'lon'), may hold values from 1 to 32
- sat_targets: int32 [4, 128, 2], P('lat', 'lon'), may hold values from 0 to 7, all different within a row; in each aligned block of 16 rows (0 to 15, 16 to 31, ..., all dimensions but the last counted through in order) at most 8 rows name the same one
Outputs:
- analysis: float32 [4, 8, 512, 1024], P('lat', 'lon')
Inputs may be any that keep to these rules, and one draw needn't show every extreme that they name: `sat_targets`: each tile names 2 different blocks. The tiles of one device name one block at most 8 times in all, and some device names some block exactly 8 times.
All inputs are finite; a program needn't handle non-finite values.
Results may differ from a plain program's by a relative error of at most 0.0073.
Values may be sent and summed in bfloat16 or wider, within the bound.
A program may use at most 128 MiB of HBM per device.

v0:
```python
import jax
import jax.numpy as jnp
from jax import lax
from jax.sharding import PartitionSpec as P

BLK = 16
LOC = 2
NS_ITERS = 3


def extended(block, sides, width, periodic):
    for axis, dim in sides:
        count = lax.axis_size(axis)
        forward = [(i, i + 1) for i in range(count - 1)]
        if periodic:
            forward.append((count - 1, 0))
        backward = [(target, source) for source, target in forward]
        low = lax.ppermute(
            lax.slice_in_dim(block, block.shape[dim] - width, None, axis=dim), axis, forward
        )
        high = lax.ppermute(lax.slice_in_dim(block, 0, width, axis=dim), axis, backward)
        block = jnp.concatenate([low, block, high], axis=dim)
    return block


def local_weight(column, lat_shift, lon_shift):
    lat_place = BLK * lat_shift + (column // BLK).astype(jnp.float32) + 0.5 - 0.5 * BLK
    lon_place = BLK * lon_shift + (column % BLK).astype(jnp.float32) + 0.5 - 0.5 * BLK
    return jnp.exp(-(lat_place * lat_place + lon_place * lon_place) / (2.0 * BLK * BLK))


def analyse(gram_sum, drive_sum, ensemble):
    members = ensemble.shape[0]
    highest = lax.Precision.HIGHEST
    identity = jnp.eye(members, dtype=jnp.float32)
    system = (members - 1.0) * identity + gram_sum
    scale = jnp.sqrt(jnp.sum(system * system))
    iterate = system / scale
    inverse_root = identity
    for sweep_index in range(NS_ITERS):
        middle = 1.5 * identity - 0.5 * jnp.dot(inverse_root, iterate, precision=highest)
        iterate = jnp.dot(iterate, middle, precision=highest)
        inverse_root = jnp.dot(middle, inverse_root, precision=highest)
    covariance = jnp.dot(inverse_root, inverse_root, precision=highest) / scale
    mean_weight = jnp.dot(covariance, drive_sum, precision=highest)
    transform = (jnp.sqrt((members - 1.0) / scale) * inverse_root + mean_weight[:, None]).astype(
        jnp.bfloat16
    )
    state_mean = jnp.mean(ensemble.astype(jnp.float32), axis=0)
    anomaly = (ensemble.astype(jnp.float32) - state_mean).astype(jnp.bfloat16)
    return state_mean + lax.dot_general(
        transform, anomaly, (((0,), (0,)), ((), ())), preferred_element_type=jnp.float32
    )


def outer_sum(scaled, spread):
    return lax.dot_general(
        scaled, spread, (((0,), (0,)), ((), ())), preferred_element_type=jnp.float32
    )


def conv_terms(nearby, conv_obs, members):
    pert_span = conv_obs * members
    spread = nearby[:, :, :pert_span].reshape(3, 3, conv_obs, members)
    misfit = nearby[:, :, pert_span : pert_span + conv_obs]
    column = nearby[:, :, pert_span + conv_obs :].astype(jnp.int32)
    shifts = jnp.arange(3).astype(jnp.float32) - 1.0
    weight = local_weight(column, shifts[:, None, None], shifts[None, :, None])
    scaled = (weight[..., None] * spread).astype(jnp.bfloat16).reshape(-1, members)
    gram_part = outer_sum(scaled, spread.reshape(-1, members))
    drive_part = jnp.dot(misfit.reshape(-1), scaled, preferred_element_type=jnp.float32)
    return (gram_part, drive_part)


def shards(
    background, conv_pert, conv_misfit, conv_column, sat_pert, sat_misfit, sat_rows, sat_targets
):
    members = background.shape[2]
    my_block = lax.axis_index("lon")
    conv_obs = conv_pert.shape[2]
    packed = jnp.concatenate(
        [conv_pert.reshape(1, 1, -1), conv_misfit, conv_column.astype(jnp.bfloat16)], axis=2
    )
    widened = extended(packed, (("lon", 1),), 1, True)
    nearby = extended(widened, (("lat", 0),), 1, False)
    gram_conv, drive_conv = conv_terms(nearby, conv_obs, members)
    entry_weight = 0.5 ** jnp.arange(LOC).astype(jnp.float32)
    obs_per_tile = sat_pert.shape[2]
    obs_index = jnp.arange(obs_per_tile)
    spread = lax.all_gather(sat_pert, "lon", axis=1, tiled=True)
    misfit = lax.all_gather(sat_misfit, "lon", axis=1, tiled=True)
    live_rows = lax.all_gather(sat_rows, "lon", axis=1, tiled=True)
    targets = lax.all_gather(sat_targets, "lon", axis=1, tiled=True)
    hit_weight = jnp.sum(jnp.where(targets == my_block, entry_weight, 0.0), axis=-1)
    keep_rows = jnp.where(obs_index < live_rows[..., None], hit_weight[..., None], 0.0)
    scaled = (keep_rows[..., None] * spread).astype(jnp.bfloat16).reshape(-1, members)
    gram_part = outer_sum(scaled, spread.reshape(-1, members))
    drive_part = jnp.dot(misfit.reshape(-1), scaled, preferred_element_type=jnp.float32)
    result = analyse(gram_conv + gram_part, drive_conv + drive_part, background[0, 0])
    return result[None, None]


def solution(mesh):
    placed = (
        P("lat", "lon", None, None),
        P("lat", "lon", None, None),
        P("lat", "lon", None),
        P("lat", "lon", None),
        P("lat", "lon", None, None),
        P("lat", "lon", None),
        P("lat", "lon"),
        P("lat", "lon", None),
    )
    return jax.shard_map(
        shards, mesh=mesh, in_specs=placed, out_specs=P("lat", "lon", None, None), check_vma=False
    )
```

profile of v0, /device:TPU:0, one launch (start us, length us, event | category | flops | bytes accessed | tf_op | source)
XLA Modules:
  0.0 126.8 jit_solution(4351079286686592873)
XLA Ops:
  7.3 1.0 reshape.100
  8.3 0.9 pad_maximum_fusion.2
  9.3 4.5 %collective-permute-start.1 = (bf16[1,1,65792]{2,1,0:T(2,128)(2,1)S(1)}, bf16[1,1,65792]{2,1,0:T(2,128)(2,1)S(1)}, u32[]{:S(2)}, u32[]{:S(2)}) collective-permute-start(bf16[1,1,65792]{2,1,0:T(2,128)(2,1)S(1)} %pad_maximum_fusion.2), channel_id=1, source_target_pairs={{1,0},{2,1},{3,2},{4,3},{5,4},{6,5},{7,6},{0,7},{9,8},{10,9},{11,1... | collective-permute-start | bytes 394760 | tf_op jit(solution)/shard_map/ppermute | solution.py:21
  13.8 2.1 %copy.12 = bf16[1,16,32,512]{3,1,2,0:T(8,128)(2,1)} copy(bf16[1,16,32,512]{3,2,1,0:T(8,128)(2,1)} %param.12) | data formatting | bytes 1048576 | tf_op args[4]
  17.6 1.0 collective-permute-done.1
  18.6 2.9 %collective-permute-done = bf16[1,1,65792]{2,1,0:T(2,128)(2,1)S(1)} collective-permute-done((bf16[1,1,65792]{2,1,0:T(2,128)(2,1)S(1)}, bf16[1,1,65792]{2,1,0:T(2,128)(2,1)S(1)}, u32[]{:S(2)}, u32[]{:S(2)}) %collective-permute-start) | collective-permute-done | bytes 131616 | tf_op jit(solution)/shard_map/ppermute | solution.py:18
  22.4 1.3 %collective-permute-start.3 = (bf16[1,3,65792]{2,1,0:T(4,128)(2,1)S(1)}, bf16[1,3,65792]{2,1,0:T(4,128)(2,1)S(1)}, u32[]{:S(2)}, u32[]{:S(2)}) collective-permute-start(bf16[1,3,65792]{2,1,0:T(4,128)(2,1)S(1)} %pad_maximum_fusion.1), channel_id=1, source_target_pairs={{8,0},{16,8},{24,16},{9,1},{17,9},{25,17},{10,2},{18,10},{26,18},{... | collective-permute-start | bytes 1184264 | tf_op jit(solution)/shard_map/ppermute | solution.py:21
  23.7 4.6 %collective-permute-start.2 = (bf16[1,3,65792]{2,1,0:T(4,128)(2,1)S(1)}, bf16[1,3,65792]{2,1,0:T(4,128)(2,1)S(1)}, u32[]{:S(2)}, u32[]{:S(2)}) collective-permute-start(bf16[1,3,65792]{2,1,0:T(4,128)(2,1)S(1)} %pad_maximum_fusion.1), channel_id=1, source_target_pairs={{0,8},{8,16},{16,24},{1,9},{9,17},{17,25},{2,10},{10,18},{18,26},{... | collective-permute-start | bytes 1184264 | tf_op jit(solution)/shard_map/ppermute | solution.py:18
  28.4 14.2 %all_gather.15 = bf16[1,128,32]{2,1,0:T(8,128)(2,1)S(1)} all-gather(bf16[1,16,32]{2,1,0:T(8,128)(2,1)S(1)} %copy-done.13), channel_id=1, replica_groups=mesh['lat'=4,'lon'=8] {'lon'}, dimensions={1}, use_global_device_ids=true | all-gather | bytes 9216 | tf_op jit(solution)/shard_map/all_gather | solution.py:91
  42.7 14.1 %all_gather.13 = s32[1,128,2]{2,0,1:T(1,128)S(1)} all-gather(s32[1,16,2]{2,0,1:T(1,128)S(1)} %copy.11), channel_id=1, replica_groups=mesh['lat'=4,'lon'=8] {'lon'}, dimensions={1}, use_global_device_ids=true | all-gather | bytes 1152 | tf_op jit(solution)/shard_map/all_gather | solution.py:93
  56.9 7.3 %all-reduce = s32[128]{0:T(128)S(1)} all-reduce(s32[128]{0:T(128)S(1)} %bitcast_dynamic-update-slice_fusion), channel_id=1, replica_groups=mesh['lat'=4,'lon'=8] {'lon'}, use_global_device_ids=true, to_apply=%add | all-reduce | flops 128 | bytes 1024
  64.1 1.0 fusion.22
  66.4 3.2 %mul.83 = f32[3,3,65536]{2,1,0:T(4,128)} reshape(f32[3,3,128,512]{3,2,1,0:T(8,128)S(1)} %mul.82) | data formatting | bytes 4718592 | tf_op jit(solution)/shard_map/mul | solution.py:69
  69.5 3.4 %pad_maximum_fusion = bf16[3,3,65792]{2,1,0:T(4,128)(2,1)S(1)} fusion(bf16[1,3,65792]{2,1,0:T(4,128)(2,1)S(1)} %collective-permute-done.3, bf16[1,1,65792]{2,1,0:T(2,128)(2,1)S(1)} %collective-permute-done.1, bf16[1,1,128]{2,1,0:T(2,128)(2,1)S(1)} %convert_element_type.69, bf16[1,1,128]{2,1,0:T(2,128)(2,1)S(1)} %copy-done.12, ...), kind=kLoop, calls=%fused_computation.15 | loop fusion | flops 8289792 | bytes 2368512 | tf_op jit(solution)/shard_map/concatenate | solution.py:22
  73.0 2.1 %slice_convert_fusion = (f32[3,3,65536]{2,1,0:T(4,128)S(1)}, bf16[3,3,65536]{2,1,0:T(4,128)(2,1)}) fusion(bf16[3,3,65792]{2,1,0:T(4,128)(2,1)S(1)} %pad_maximum_fusion), kind=kLoop, calls=%fused_computation.68 | loop fusion | flops 589824 | bytes 4718592 | tf_op jit(solution)/shard_map/convert_element_type | solution.py:69
  75.2 2.1 %multiply_convert_fusion.1 = bf16[3,3,65536]{2,1,0:T(4,128)(2,1)} fusion(f32[3,3,65536]{2,1,0:T(4,128)S(1)} %copy-done, bf16[3,3,65792]{2,1,0:T(4,128)(2,1)S(1)} %pad_maximum_fusion), kind=kLoop, calls=%fused_computation.5 | loop fusion | flops 1769472 | bytes 4718592 | tf_op jit(solution)/shard_map/convert_element_type | solution.py:69
  77.2 4.0 %convert_element_type.75 = bf16[1152,512]{1,0:T(8,128)(2,1)} reshape(bf16[3,3,65536]{2,1,0:T(4,128)(2,1)} %multiply_convert_fusion.1) | data formatting | bytes 2359296 | tf_op jit(solution)/shard_map/convert_element_type | solution.py:69
  81.2 3.0 %reshape.104 = f32[3,3,128,512]{3,2,1,0:T(8,128)} reshape(f32[3,3,65536]{2,1,0:T(4,128)S(1)} %get-tuple-element.5) | data formatting | bytes 4718592 | tf_op jit(solution)/shard_map/convert_element_type | solution.py:69
  84.2 4.2 %reshape_reshape.3 = bf16[1152,512]{1,0:T(8,128)(2,1)} reshape(bf16[3,3,65536]{2,1,0:T(4,128)(2,1)} %get-tuple-element.6) | data formatting | bytes 2359296 | tf_op jit(solution)/shard_map/reshape;reshape | solution.py:70
  89.5 6.1 %fusion.8 = f32[512,512]{1,0:T(8,128)S(1)} fusion(bf16[1,128,32,512]{3,1,2,0:T(8,128)(2,1)} %all-gather.2.cloned.1.call-done, f32[128,32]{0,1:T(8,128)S(1)} %fusion.23), kind=kOutput, calls=%fused_computation.16 | convolution fusion | flops 2153775104 | bytes 5259264 | tf_op jit(solution)/shard_map/dot_general | solution.py:57
  95.6 2.5 %multiply_reduce_fusion = (f32[]{:T(128)}, f32[512,512]{1,0:T(8,128)}) fusion(f32[512,512]{1,0:T(8,128)S(1)} %fusion.8, bf16[1152,512]{1,0:T(8,128)(2,1)S(1)} %copy-done.8, bf16[1152,512]{1,0:T(8,128)(2,1)S(1)} %copy-done.9), kind=kOutput, calls=%fused_computation.26 | convolution fusion | flops 605552640 | bytes 4456452 | tf_op jit(solution)/shard_map/dot_general | solution.py:57
  98.8 2.4 %select_subtract_fusion.2 = f32[512,512]{1,0:T(8,128)S(1)} fusion(f32[512,512]{1,0:T(8,128)} %get-tuple-element.8, f32[]{:T(128)S(6)} %sqrt.6), kind=kOutput, calls=%fused_computation.14 | convolution fusion | flops 1612185600 | bytes 2097156 | tf_op jit(solution)/shard_map/dot_general | solution.py:41
  101.3 1.9 %fusion.21 = f32[512,512]{1,0:T(8,128)S(1)} fusion(f32[512,512]{1,0:T(8,128)S(1)} %select_subtract_fusion.2, f32[512,512]{1,0:T(8,128)S(1)} %copy-done.18, f32[]{:T(128)S(6)} %sqrt.6), kind=kOutput, calls=%fused_computation.34 | convolution fusion | flops 1610874880 | bytes 3145732 | tf_op jit(solution)/shard_map/dot_general | solution.py:42
  103.1 1.0 fusion.17
  104.1 1.8 %select_subtract_fusion.1 = f32[512,512]{1,0:T(8,128)S(1)} fusion(f32[512,512]{1,0:T(8,128)S(1)} %fusion.17, f32[512,512]{1,0:T(8,128)S(1)} %fusion.21), kind=kOutput, calls=%fused_computation.13 | convolution fusion | flops 1611661312 | bytes 3145728 | tf_op jit(solution)/shard_map/dot_general | solution.py:41
  106.0 1.8 %fusion.38 = f32[512,512]{1,0:T(8,128)S(1)} fusion(f32[512,512]{1,0:T(8,128)S(1)} %select_subtract_fusion.1, f32[512,512]{1,0:T(8,128)S(1)} %fusion.17), kind=kOutput, calls=%fused_computation.69 | convolution fusion | flops 1610612736 | bytes 3145728 | tf_op jit(solution)/shard_map/dot_general | solution.py:43
  107.8 2.1 %fusion.39 = f32[512,512]{1,0:T(8,128)S(1)} fusion(f32[512,512]{1,0:T(8,128)S(1)} %fusion.21, f32[512,512]{1,0:T(8,128)S(1)} %select_subtract_fusion.1), kind=kOutput, calls=%fused_computation.70 | convolution fusion | flops 1610612736 | bytes 3145728 | tf_op jit(solution)/shard_map/dot_general | solution.py:42
  110.0 1.8 %select_subtract_fusion = f32[512,512]{1,0:T(8,128)S(1)} fusion(f32[512,512]{1,0:T(8,128)S(1)} %fusion.38, f32[512,512]{1,0:T(8,128)S(1)} %fusion.39), kind=kOutput, calls=%fused_computation.12 | convolution fusion | flops 1611661312 | bytes 3145728 | tf_op jit(solution)/shard_map/dot_general | solution.py:41
  111.9 1.9 %fusion.40 = f32[512,512]{1,0:T(8,128)S(1)} fusion(f32[512,512]{1,0:T(8,128)S(1)} %select_subtract_fusion, f32[512,512]{1,0:T(8,128)S(1)} %fusion.38), kind=kOutput, calls=%fused_computation.71 | convolution fusion | flops 1610612736 | bytes 3145728 | tf_op jit(solution)/shard_map/dot_general | solution.py:43
  113.7 1.9 %convolution_divide_fusion = f32[512,512]{1,0:T(8,128)S(1)} fusion(f32[512,512]{1,0:T(8,128)S(1)} %fusion.40, f32[]{:T(128)S(6)} %sqrt.6), kind=kOutput, calls=%fused_computation.17 | convolution fusion | flops 1610874880 | bytes 2097156 | tf_op jit(solution)/shard_map/dot_general | solution.py:44
  116.8 1.0 fusion.41
  117.8 2.2 %add_bitcast_fusion = f32[1,1,512,1024]{3,2,1,0:T(8,128)} fusion(bf16[1,1,512,1024]{3,2,1,0:T(8,128)(2,1)S(1)} %copy-done.11, f32[1024]{0:T(1024)S(1)} %broadcast_multiply_fusion, f32[512,512]{1,0:T(8,128)S(1)} %fusion.40, f32[512]{0:T(512)S(1)} %bitcast.61, f32[]{:T(128)S(6)} %sqrt.7), kind=kOutput, calls=%fused_computation.11 | convolution fusion | flops 539754496 | bytes 4200452 | tf_op jit(solution)/shard_map/dot_general | solution.py:51
  (62 shorter events, 6.3 us)
Async XLA Ops:
  6.5 9.6 %copy-start.17 = (u32[32]{0:T(128)S(1)}, u32[32]{0:T(128)}, u32[]{:S(2)}) copy-start(u32[32]{0:T(128)} %constant.72) | copy-start | bytes 388
  6.5 15.0 %copy-start.12 = (bf16[1,1,128]{2,1,0:T(2,128)(2,1)S(1)}, bf16[1,1,128]{2,1,0:T(2,128)(2,1)}, u32[]{:S(2)}) copy-start(bf16[1,1,128]{2,1,0:T(2,128)(2,1)} %param.10) | copy-start | bytes 772
  6.5 9.4 %copy-start.10 = (bf16[1,1,512,1024]{3,2,1,0:T(8,128)(2,1)S(1)}, bf16[1,1,512,1024]{3,2,1,0:T(8,128)(2,1)}, u32[]{:S(2)}) copy-start(bf16[1,1,512,1024]{3,2,1,0:T(8,128)(2,1)} %param.8) | copy-start | bytes 3145732
  6.5 10.9 %copy-start.16 = (s32[1,16]{1,0:T(1,128)S(1)}, s32[1,16]{1,0:T(1,128)}, u32[]{:S(2)}) copy-start(s32[1,16]{1,0:T(1,128)} %param.14) | copy-start | bytes 196
  6.5 82.9 %all-gather.2.cloned.1.call-start = ((), (), s32[]{:S(2)}) async-start(), calls=%async_computation | async-start | bytes 4718592 | tf_op jit(solution)/shard_map/all_gather | solution.py:90
  9.2 19.1 %copy-start.14 = (s32[1,16,2]{1,2,0:T(2,128)S(1)}, s32[1,16,2]{1,2,0:T(2,128)}, u32[]{:S(2)}) copy-start(s32[1,16,2]{1,2,0:T(2,128)} %param.15) | copy-start | bytes 388
  9.2 19.2 %copy-start.13 = (bf16[1,16,32]{2,1,0:T(8,128)(2,1)S(1)}, bf16[1,16,32]{2,1,0:T(8,128)(2,1)}, u32[]{:S(2)}) copy-start(bf16[1,16,32]{2,1,0:T(8,128)(2,1)} %param.13) | copy-start | bytes 3076
  9.3 9.3 %collective-permute-start.1 = (bf16[1,1,65792]{2,1,0:T(2,128)(2,1)S(1)}, bf16[1,1,65792]{2,1,0:T(2,128)(2,1)S(1)}, u32[]{:S(2)}, u32[]{:S(2)}) collective-permute-start(bf16[1,1,65792]{2,1,0:T(2,128)(2,1)S(1)} %pad_maximum_fusion.2), channel_id=1, source_target_pairs={{1,0},{2,1},{3,2},{4,3},{5,4},{6,5},{7,6},{0,7},{9,8},{10,9},{11,1... | collective-permute-start | bytes 394760 | tf_op jit(solution)/shard_map/ppermute | solution.py:21
  13.8 7.7 %collective-permute-start = (bf16[1,1,65792]{2,1,0:T(2,128)(2,1)S(1)}, bf16[1,1,65792]{2,1,0:T(2,128)(2,1)S(1)}, u32[]{:S(2)}, u32[]{:S(2)}) collective-permute-start(bf16[1,1,65792]{2,1,0:T(2,128)(2,1)S(1)} %pad_maximum_fusion.2), channel_id=1, source_target_pairs={{0,1},{1,2},{2,3},{3,4},{4,5},{5,6},{6,7},{7,0},{8,9},{9,10},{10,1... | collective-permute-start | bytes 394760 | tf_op jit(solution)/shard_map/ppermute | solution.py:18
  18.6 50.9 %copy-start.5 = (bf16[1,1,65792]{2,1,0:T(2,128)(2,1)}, bf16[1,1,65792]{2,1,0:T(2,128)(2,1)S(1)}, u32[]{:S(2)}) copy-start(bf16[1,1,65792]{2,1,0:T(2,128)(2,1)S(1)} %collective-permute-done.1) | copy-start | bytes 394756
  21.6 43.6 %copy-start.7 = (bf16[1,1,65792]{2,1,0:T(2,128)(2,1)}, bf16[1,1,65792]{2,1,0:T(2,128)(2,1)S(1)}, u32[]{:S(2)}) copy-start(bf16[1,1,65792]{2,1,0:T(2,128)(2,1)S(1)} %collective-permute-done) | copy-start | bytes 394756
  22.4 42.7 %collective-permute-start.3 = (bf16[1,3,65792]{2,1,0:T(4,128)(2,1)S(1)}, bf16[1,3,65792]{2,1,0:T(4,128)(2,1)S(1)}, u32[]{:S(2)}, u32[]{:S(2)}) collective-permute-start(bf16[1,3,65792]{2,1,0:T(4,128)(2,1)S(1)} %pad_maximum_fusion.1), channel_id=1, source_target_pairs={{8,0},{16,8},{24,16},{9,1},{17,9},{25,17},{10,2},{18,10},{26,18},{... | collective-permute-start | bytes 1184264 | tf_op jit(solution)/shard_map/ppermute | solution.py:21
  23.7 41.4 %collective-permute-start.2 = (bf16[1,3,65792]{2,1,0:T(4,128)(2,1)S(1)}, bf16[1,3,65792]{2,1,0:T(4,128)(2,1)S(1)}, u32[]{:S(2)}, u32[]{:S(2)}) collective-permute-start(bf16[1,3,65792]{2,1,0:T(4,128)(2,1)S(1)} %pad_maximum_fusion.1), channel_id=1, source_target_pairs={{0,8},{8,16},{16,24},{1,9},{9,17},{17,25},{2,10},{10,18},{18,26},{... | collective-permute-start | bytes 1184264 | tf_op jit(solution)/shard_map/ppermute | solution.py:18
  65.2 4.4 %copy-start.2 = (bf16[1,3,65792]{2,1,0:T(4,128)(2,1)}, bf16[1,3,65792]{2,1,0:T(4,128)(2,1)S(1)}, u32[]{:S(2)}) copy-start(bf16[1,3,65792]{2,1,0:T(4,128)(2,1)S(1)} %collective-permute-done.3) | copy-start | bytes 1184260
  65.2 0.9 copy-start.4
  73.0 2.2 %copy-start = (f32[3,3,65536]{2,1,0:T(4,128)S(1)}, f32[3,3,65536]{2,1,0:T(4,128)}, u32[]{:S(2)}) copy-start(f32[3,3,65536]{2,1,0:T(4,128)} %mul.83) | copy-start | bytes 7077892
  84.2 4.2 %copy-start.3 = (bf16[1,3,65792]{2,1,0:T(4,128)(2,1)S(1)}, bf16[1,3,65792]{2,1,0:T(4,128)(2,1)}, u32[]{:S(2)}) copy-start(bf16[1,3,65792]{2,1,0:T(4,128)(2,1)} %copy-done.2) | copy-start | bytes 1184260
  84.2 4.2 %copy-start.6 = (bf16[1,1,65792]{2,1,0:T(2,128)(2,1)S(1)}, bf16[1,1,65792]{2,1,0:T(2,128)(2,1)}, u32[]{:S(2)}) copy-start(bf16[1,1,65792]{2,1,0:T(2,128)(2,1)} %copy-done.5) | copy-start | bytes 394756
  84.2 4.9 %copy-start.1 = (f32[3,3,128,512]{3,2,1,0:T(8,128)S(1)}, f32[3,3,128,512]{3,2,1,0:T(8,128)}, u32[]{:S(2)}) copy-start(f32[3,3,128,512]{3,2,1,0:T(8,128)} %reshape.104) | copy-start | bytes 7077892
  89.4 6.1 %copy-start.8 = (bf16[1152,512]{1,0:T(8,128)(2,1)S(1)}, bf16[1152,512]{1,0:T(8,128)(2,1)}, u32[]{:S(2)}) copy-start(bf16[1152,512]{1,0:T(8,128)(2,1)} %convert_element_type.75) | copy-start | bytes 3538948
  89.5 6.1 %copy-start.9 = (bf16[1152,512]{1,0:T(8,128)(2,1)S(1)}, bf16[1152,512]{1,0:T(8,128)(2,1)}, u32[]{:S(2)}) copy-start(bf16[1152,512]{1,0:T(8,128)(2,1)} %reshape_reshape.3) | copy-start | bytes 3538948
  98.8 2.4 %copy-start.18 = (f32[512,512]{1,0:T(8,128)S(1)}, f32[512,512]{1,0:T(8,128)}, u32[]{:S(2)}) copy-start(f32[512,512]{1,0:T(8,128)} %get-tuple-element.8) | copy-start | bytes 3145732
  113.7 2.2 %copy-start.15 = (bf16[1,128,32,512]{3,1,2,0:T(8,128)(2,1)S(1)}, bf16[1,128,32,512]{3,1,2,0:T(8,128)(2,1)}, u32[]{:S(2)}) copy-start(bf16[1,128,32,512]{3,1,2,0:T(8,128)(2,1)} %all-gather.2.cloned.1.call-done) | copy-start | bytes 12582916
  115.9 1.9 %copy-start.11 = (bf16[1,1,512,1024]{3,2,1,0:T(8,128)(2,1)S(1)}, bf16[1,1,512,1024]{3,2,1,0:T(8,128)(2,1)}, u32[]{:S(2)}) copy-start(bf16[1,1,512,1024]{3,2,1,0:T(8,128)(2,1)} %param.8) | copy-start | bytes 3145732
Sparse Core Ops, SparseCore 0:
  16.1 49.1 all-gather.1
where the time goes:
time: 127 us
  blocking collectives  35.6 us (28%)
  matrix products  29.6 us (23%)
  local copies, waits for them, and re-layouts  19.9 us (16%)
  between operations  15.2 us (12%)
  other arithmetic  12.1 us (10%)
  starting transfers between devices  10.4 us (8%)
  waiting for transfers between devices  4.01 us (3%)
    all_gather x1, blocking collectives, shards(): misfit = lax.all_gather(sat_misfit, 'lon', axis=1, tiled=True)  14.2 us
    all_gather x1, blocking collectives, shards(): targets = lax.all_gather(sat_targets, 'lon', axis=1, tiled=True)  14.1 us
    dot_general x2, matrix products, outer_sum(): lax.dot_general(scaled, spread, (((0,), (0,)), ((), ())), preferred_eleme...  8.61 us
    unnamed x1, blocking collectives  7.28 us
    dot_general x3, matrix products, analyse(): jnp.dot(inverse_root, iterate, precision=highest)  6.1 us
    ppermute x2, starting transfers between devices, extended(): lax.ppermute(lax.slice_in_dim(block, 0, width, axis=dim), axis, backward)  5.83 us
    dot_general x3, matrix products, analyse(): inverse_root = jnp.dot(middle, inverse_root, precision=highest)  4.68 us
    ppermute x2, starting transfers between devices, extended(): lax.ppermute(lax.slice_in_dim(block, block.shape[dim] - width, None, axis...  4.58 us
  transfers between devices with their start and end apart: 5, of which 2 were waited for; matrix products, arithmetic and copies ran while one was open for 22% of the time, Pallas kernels for 0%

commit v1 on v0

v1 whole, which is shorter than its diff:
```python
import functools

import jax
import jax.numpy as jnp
from jax import lax
from jax.experimental import pallas as pl
from jax.experimental.pallas import tpu as pltpu
from jax.sharding import PartitionSpec as P

BLK = 16
MESH = pl.DeviceIdType.MESH
F32 = jnp.float32
BF16 = jnp.bfloat16
EXTRA = 16


def dot(left, right):
    return lax.dot_general(left, right, (((1,), (0,)), ((), ())), preferred_element_type=F32)


def iota(shape, dim):
    return lax.broadcasted_iota(jnp.int32, shape, dim)


def gather_kernel(
    n_lat, n_lon,
    conv_pert, conv_misfit, conv_column, sat_pert, sat_misfit, sat_rows, sat_targets,
    out,
    sat_buf, conv_buf, sat_flip, conv_flip, acc, send_buf, recv_buf,
    sat_send, sat_recv, conv_send, conv_recv, line_send, line_recv,
):
    chips = n_lon // 2
    band = lax.axis_index("lat")
    block = lax.axis_index("lon")
    chip, core = block // 2, block % 2
    sibling = 2 * chip + (1 - core)
    tiles, tile_obs = sat_misfit.shape[1], sat_misfit.shape[2]
    rows, members = tiles * tile_obs, sat_pert.shape[3]
    conv_obs = conv_pert.shape[2]
    half = members // 2
    has_north, has_south = band > 0, band < n_lat - 1
    has_low, has_high = chip > 0, chip < chips - 1
    mates = (
        (has_north, (band - 1, block)),
        (has_south, (band + 1, block)),
        (has_low, (band, block - 2)),
        (has_high, (band, block + 2)),
    )

    conv_buf[0, 1, :conv_obs, :] = conv_pert[0, 0]
    conv_buf[0, 1, conv_obs:, :] = jnp.concatenate(
        [
            jnp.broadcast_to(conv_column[0].astype(F32).astype(BF16), (EXTRA, conv_obs)),
            jnp.broadcast_to(conv_misfit[0], (EXTRA, conv_obs)),
            jnp.zeros((EXTRA, members - 2 * conv_obs), BF16),
        ],
        axis=1,
    )

    own_tile = iota((tiles, rows), 1) // tile_obs == iota((tiles, rows), 0)
    spread_obs = (iota((tile_obs, rows), 1) % tile_obs == iota((tile_obs, rows), 0)).astype(BF16)
    misfit = jnp.sum(jnp.where(own_tile, dot(sat_misfit[0], spread_obs), 0.0), axis=0, keepdims=True)
    count = dot(
        jnp.broadcast_to(sat_rows[...].astype(F32).astype(BF16), (8, tiles)), own_tile.astype(BF16)
    )[0:1]
    live = (iota((1, rows), 1) % tile_obs).astype(F32) < count
    names = sat_targets[0].astype(F32)
    lists = [
        jnp.where(
            live,
            jnp.sum(jnp.where(own_tile, names[:, e : e + 1], 0.0), axis=0, keepdims=True),
            -1.0,
        )
        for e in range(2)
    ]
    place = iota((EXTRA, rows), 0)
    sat_buf[0, :rows, :] = sat_pert[0].reshape(rows, members)
    sat_buf[0, rows:, :] = jnp.where(
        place == 0, lists[0], jnp.where(place == 1, lists[1], jnp.where(place == 2, misfit, 0.0))
    ).astype(BF16)

    barrier = pltpu.get_barrier_semaphore()
    pl.semaphore_signal(barrier, inc=1, device_id=(band, sibling), device_id_type=MESH)
    for here, mate in mates:
        @pl.when(here)
        def _():
            pl.semaphore_signal(barrier, inc=1, device_id=mate, device_id_type=MESH)
    pl.semaphore_wait(barrier, 1 + sum(here.astype(jnp.int32) for here, _ in mates))

    sat_copy = pltpu.make_async_remote_copy(
        src_ref=sat_buf.at[0], dst_ref=sat_buf.at[1], send_sem=sat_send, recv_sem=sat_recv,
        device_id=(band, sibling), device_id_type=MESH,
    )
    sat_copy.start()

    def conv_copy(group, slot, to_group, to_slot, sem, mate):
        return pltpu.make_async_remote_copy(
            src_ref=conv_buf.at[group, slot], dst_ref=conv_buf.at[to_group, to_slot],
            send_sem=conv_send.at[sem], recv_sem=conv_recv.at[sem],
            device_id=mate, device_id_type=MESH,
        )

    to_north = conv_copy(0, 1, 0, 2, 0, (band - 1, block))
    to_south = conv_copy(0, 1, 0, 0, 1, (band + 1, block))
    to_side = conv_copy(0, 1, 1, 1, 2, (band, sibling))
    relays = [conv_copy(0, 0, 1, 0, 3, (band, sibling)), conv_copy(0, 2, 1, 2, 4, (band, sibling))]
    blank = jnp.zeros((conv_obs + EXTRA, members), BF16)

    @pl.when(has_north)
    def _():
        to_north.start()

    @pl.when(has_south)
    def _():
        to_south.start()

    to_side.start()

    @pl.when(jnp.logical_not(has_north))
    def _():
        conv_buf[0, 0] = blank
        conv_buf[1, 0] = blank

    @pl.when(jnp.logical_not(has_south))
    def _():
        conv_buf[0, 2] = blank
        conv_buf[1, 2] = blank

    def flip_sat(side):
        sat_flip[:, pl.ds(side * rows, rows)] = sat_buf[side, :rows, :].T

    flip_sat(0)
    sat_copy.wait_recv()
    flip_sat(1)

    def relay():
        @pl.when(has_north)
        def _():
            to_south.wait_recv()
            relays[0].start()

        @pl.when(has_south)
        def _():
            to_north.wait_recv()
            relays[1].start()

    def conv_ready():
        to_side.wait_recv()

        @pl.when(has_north)
        def _():
            relays[0].wait_recv()

        @pl.when(has_south)
        def _():
            relays[1].wait_recv()

        for group in range(2):
            for slot in range(3):
                at = (group * 3 + slot) * conv_obs
                conv_flip[:, at : at + conv_obs] = conv_buf[group, slot, :conv_obs, :].T

    def conv_weight(group, slot, target):
        column = conv_buf[group, slot, conv_obs:, :conv_obs][0:1].astype(F32)
        source = block if group == 0 else sibling
        away = lax.rem(source - target + 1 + n_lon, n_lon) - 1
        row = jnp.floor(column * (1.0 / BLK))
        lat_place = BLK * (slot - 1.0) + row + 0.5 - 0.5 * BLK
        lon_place = BLK * away.astype(F32) + (column - BLK * row) + 0.5 - 0.5 * BLK
        weight = jnp.exp(-(lat_place * lat_place + lon_place * lon_place) / (2.0 * BLK * BLK))
        return jnp.where(away <= 1, weight, 0.0)

    place = iota((EXTRA, members), 0)
    eye = iota((half, half), 0) == iota((half, half), 1)
    upper = iota((half, half), 0) <= iota((half, half), 1)

    def add_terms(slot, scaled, spread, forced, first):
        top = dot(scaled[:half], spread)
        low = dot(scaled[half:], spread[:, half:])
        drive = dot(forced, spread)
        diagonal = jnp.sum(jnp.where(eye, low, 0.0), axis=0, keepdims=True)
        packed = jnp.where(upper, top[:, :half], low)
        tail = jnp.where(place == 0, drive[0:1], 0.0) + jnp.where(
            place == 2, jnp.concatenate([diagonal, jnp.zeros_like(diagonal)], axis=1), 0.0
        )
        if first:
            acc[slot, :half, :half] = packed
            acc[slot, :half, half:] = top[:, half:]
            acc[slot, half:, :] = tail
        else:
            acc[slot, :half, :half] += packed
            acc[slot, :half, half:] += top[:, half:]
            acc[slot, half:, :] += tail

    def compute(slot, to_chip):
        target = 2 * to_chip + core
        name = target.astype(F32)

        weights, pushes = [], []
        for side in range(2):
            lists = sat_buf[side, rows:, :].astype(F32)
            weight = jnp.where(lists[0:1] == name, 1.0, 0.0) + jnp.where(lists[1:2] == name, 0.5, 0.0)
            weights.append(weight)
            pushes.append(weight * lists[2:3])
        weight = jnp.concatenate(weights, axis=1)
        push = jnp.concatenate(pushes, axis=1)
        scaled = sat_flip[...] * weight.astype(BF16)
        spread = jnp.concatenate([sat_buf[side, :rows, :] for side in range(2)], axis=0)
        add_terms(slot, scaled, spread, jnp.broadcast_to(push, (EXTRA, 2 * rows)).astype(BF16), True)

        near = jnp.logical_or(to_chip == chip, to_chip == wrapped)

        @pl.when(near)
        def _():
            weights, pushes, spreads = [], [], []
            for group in range(2):
                for place in range(3):
                    weight = conv_weight(group, place, target)
                    misfit = conv_buf[group, place, conv_obs:, conv_obs : 2 * conv_obs][0:1].astype(F32)
                    weights.append(weight)
                    pushes.append(weight * misfit)
                    spreads.append(conv_buf[group, place, :conv_obs, :])
            weight = jnp.concatenate(weights, axis=1)
            push = jnp.concatenate(pushes, axis=1)
            push_high = push.astype(BF16)
            scaled = (conv_flip[...].astype(F32) * weight).astype(BF16)
            spread = jnp.concatenate(spreads, axis=0)
            add_terms(slot, scaled, spread, jnp.broadcast_to(push_high, (EXTRA, 6 * conv_obs)), False)

    def line_copy(way, to_chip):
        ahead = block + 2 if way == 0 else block - 2
        return pltpu.make_async_remote_copy(
            src_ref=send_buf.at[way, to_chip], dst_ref=recv_buf.at[way, to_chip],
            send_sem=line_send.at[way, to_chip], recv_sem=line_recv.at[way, to_chip],
            device_id=(band, ahead), device_id_type=MESH,
        )

    def step_of(way, step):
        if way == 0:
            to_chip = chips - 1 + chip - step
            return to_chip, jnp.logical_and(to_chip > chip, to_chip < chips), has_low
        to_chip = step + chip - chips + 1
        return to_chip, jnp.logical_and(to_chip >= 0, to_chip < chip), has_high

    def finish(way, slot, to_chip, behind):
        @pl.when(behind)
        def _():
            line_copy(way, to_chip).wait_recv()
            acc[slot] += recv_buf[way, to_chip].astype(F32)

        value = acc[slot]
        tail = value[half:]
        high = tail[0:1].astype(BF16).astype(F32)
        kept = tail[2:3].astype(BF16).astype(F32)
        send_buf[way, to_chip, :half, :] = value[:half].astype(BF16)
        send_buf[way, to_chip, half:, :] = jnp.where(
            place == 1,
            tail[0:1] + tail[1:2] - high,
            jnp.where(place == 3, tail[2:3] + tail[3:4] - kept, tail),
        ).astype(BF16)
        line_copy(way, to_chip).start()

    def step_body(step, carry):
        for way in range(2):
            to_chip, wanted, behind = step_of(way, step)

            @pl.when(wanted)
            def _():
                @pl.when(to_chip == wrapped)
                def _():
                    conv_ready()

                compute(way, to_chip)
        for way in range(2):
            to_chip, wanted, behind = step_of(way, step)

            @pl.when(wanted)
            def _():
                finish(way, way, to_chip, behind)

        @pl.when(jnp.logical_and(step == 0, jnp.logical_not(early)))
        def _():
            relay()

        return carry

    wrapped = lax.rem(chip + 1 - 2 * core + chips, chips)
    early = jnp.logical_or(
        jnp.logical_and(jnp.logical_not(has_low), wrapped == chips - 1),
        jnp.logical_and(jnp.logical_not(has_high), wrapped == 0),
    )

    @pl.when(early)
    def _():
        relay()

    lax.fori_loop(0, chips - 1, step_body, 0)

    compute(0, chip)

    @pl.when(has_low)
    def _():
        line_copy(0, chip).wait_recv()
        acc[0] += recv_buf[0, chip].astype(F32)

    @pl.when(has_high)
    def _():
        line_copy(1, chip).wait_recv()
        acc[0] += recv_buf[1, chip].astype(F32)

    out[...] = acc[0]

    sat_copy.wait_send()
    to_side.wait_send()

    @pl.when(has_north)
    def _():
        to_north.wait_send()
        relays[0].wait_send()

    @pl.when(has_south)
    def _():
        to_south.wait_send()
        relays[1].wait_send()

    def drain(step, carry):
        for way in range(2):
            to_chip, wanted, _ = step_of(way, step)

            @pl.when(wanted)
            def _():
                line_copy(way, to_chip).wait_send()
        return carry

    lax.fori_loop(0, chips - 1, drain, 0)


def analyse_kernel(packed, background, out):
    members = background.shape[2]
    half = members // 2
    field = packed[:half, :half]
    cross = packed[:half, half:]
    drive = packed[half : half + 1] + packed[half + 1 : half + 2]
    diagonal = (packed[half + 2 : half + 3] + packed[half + 3 : half + 4])[:, :half]
    row, col = iota((half, half), 0), iota((half, half), 1)
    strict = jnp.where(row < col, field, 0.0)
    under = jnp.where(row > col, field, 0.0)
    first = jnp.where(row <= col, field, 0.0) + strict.T
    second = under + under.T + jnp.where(row == col, diagonal, 0.0)
    gram = jnp.concatenate(
        [jnp.concatenate([first, cross], axis=1), jnp.concatenate([cross.T, second], axis=1)], axis=0
    )
    one = (iota((members, members), 0) == iota((members, members), 1)).astype(F32)
    system = (members - 1.0) * one + gram
    scale = jnp.sqrt(jnp.sum(jnp.sum(system * system, axis=0, keepdims=True), axis=1, keepdims=True))
    y = system / scale
    yb = y.astype(BF16)
    square = dot(yb, yb)
    u = 1.5 * y - 0.5 * square
    w = 0.25 * square - 1.5 * y
    q = 2.25 * u + dot(u.astype(BF16), w.astype(BF16))
    e2 = -0.75 * y - 0.5 * q
    e2b = e2.astype(BF16)
    f = 2.25 * y + dot(yb, e2b)
    h = 4.5 * e2 + dot(e2b, e2b)
    e3 = 1.5 * e2 - 0.5 * (5.0625 * f + dot(f.astype(BF16), h.astype(BF16)))
    e3b = e3.astype(BF16)

    def times_root(vector):
        high = vector.astype(BF16)
        low = (vector - high.astype(F32)).astype(BF16)
        place = iota((16, members), 0)
        both = jnp.where(place == 0, high.astype(F32), jnp.where(place == 1, low.astype(F32), 0.0))
        product = dot(both.astype(BF16), e3b)
        return 3.375 * vector + product[0:1] + product[1:2]

    mean_weight = times_root(times_root(drive)) / scale
    transform = (jnp.sqrt((members - 1.0) / scale) * (3.375 * one + e3)).astype(BF16)

    ensemble = background[0, 0].astype(F32)
    state_mean = jnp.mean(ensemble, axis=0, keepdims=True)
    anomaly = (ensemble - state_mean).astype(BF16)
    high = mean_weight.astype(BF16)
    low = (mean_weight - high.astype(F32)).astype(BF16)
    place = iota((16, members), 0)
    both = jnp.where(place == 0, high.astype(F32), jnp.where(place == 1, low.astype(F32), 0.0))
    shift = dot(both.astype(BF16), anomaly)
    out[0, 0] = dot(transform, anomaly) + (state_mean + shift[0:1] + shift[1:2])


def shards(
    n_lat, n_lon,
    background, conv_pert, conv_misfit, conv_column, sat_pert, sat_misfit, sat_rows, sat_targets,
):
    members, cells = background.shape[2:]
    tiles, tile_obs = sat_pert.shape[1:3]
    conv_obs = conv_pert.shape[2]
    rows, chips, half = tiles * tile_obs, n_lon // 2, members // 2
    vmem = pl.BlockSpec(memory_space=pltpu.VMEM)
    packed = pl.pallas_call(
        functools.partial(gather_kernel, n_lat, n_lon),
        out_shape=jax.ShapeDtypeStruct((half + EXTRA, members), F32),
        in_specs=[vmem] * 7,
        out_specs=vmem,
        scratch_shapes=[
            pltpu.VMEM((2, rows + EXTRA, members), BF16),
            pltpu.VMEM((2, 3, conv_obs + EXTRA, members), BF16),
            pltpu.VMEM((members, 2 * rows), BF16),
            pltpu.VMEM((members, 6 * conv_obs), BF16),
            pltpu.VMEM((2, half + EXTRA, members), F32),
            pltpu.VMEM((2, chips, half + EXTRA, members), BF16),
            pltpu.VMEM((2, chips, half + EXTRA, members), BF16),
            pltpu.SemaphoreType.DMA,
            pltpu.SemaphoreType.DMA,
            pltpu.SemaphoreType.DMA((5,)),
            pltpu.SemaphoreType.DMA((5,)),
            pltpu.SemaphoreType.DMA((2, chips)),
            pltpu.SemaphoreType.DMA((2, chips)),
        ],
        compiler_params=pltpu.CompilerParams(
            collective_id=0, has_side_effects=True, vmem_limit_bytes=48 * 1024 * 1024
        ),
        cost_estimate=pl.CostEstimate(
            flops=2 * (chips * 2 * rows + 9 * conv_obs) * members * members,
            bytes_accessed=4 * rows * members, transcendentals=0,
        ),
        name="gather_grams",
    )(conv_pert, conv_misfit, conv_column, sat_pert, sat_misfit, sat_rows, sat_targets)
    return pl.pallas_call(
        analyse_kernel,
        out_shape=jax.ShapeDtypeStruct((1, 1, members, cells), F32),
        in_specs=[vmem] * 2,
        out_specs=vmem,
        compiler_params=pltpu.CompilerParams(vmem_limit_bytes=48 * 1024 * 1024),
        cost_estimate=pl.CostEstimate(
            flops=14 * members * members * members, bytes_accessed=6 * members * cells, transcendentals=0
        ),
        name="analyse",
    )(packed, background)


def solution(mesh):
    placed = (
        P("lat", "lon", None, None),
        P("lat", "lon", None, None),
        P("lat", "lon", None),
        P("lat", "lon", None),
        P("lat", "lon", None, None),
        P("lat", "lon", None),
        P("lat", "lon"),
        P("lat", "lon", None),
    )
    return jax.shard_map(
        functools.partial(shards, mesh.shape["lat"], mesh.shape["lon"]),
        mesh=mesh, in_specs=placed, out_specs=P("lat", "lon", None, None), check_vma=False,
    )
```

time: 127 us -> 44.2 us (0.35)
  Pallas kernels: 0 us -> 38.1 us
  blocking collectives: 35.6 us -> 0 us
  matrix products: 29.6 us -> 0 us
  between operations: 15.2 us -> 0.02 us
  local copies, waits for them, and re-layouts: 19.9 us -> 5.35 us
  other arithmetic: 12.1 us -> 0 us
  starting transfers between devices: 10.4 us -> 0 us
  waiting for transfers between devices: 4.01 us -> 0 us
    pallas_call x0 -> x2, Pallas kernels: none -> 38.1 us  [the longest x1 33.1 us: shards(): pl.pallas_call(functools.partial(gather_kernel, n_lat, n_lon), out_shape=...]
    dot_general x15 -> x0, matrix products: 29.6 us -> none  [the longest x2 8.61 us: outer_sum(): lax.dot_general(scaled, spread, (((0,), (0,)), ((), ())), preferred_eleme...]
    all_gather x2 -> x0, blocking collectives: 28.3 us -> none  [the longest x1 14.2 us: shards(): misfit = lax.all_gather(sat_misfit, 'lon', axis=1, tiled=True)]
    ppermute x4 -> x0, starting transfers between devices: 10.4 us -> none  [the longest x2 5.83 us: extended(): lax.ppermute(lax.slice_in_dim(block, 0, width, axis=dim), axis, backward)]
    unnamed x1 -> x0, blocking collectives: 7.28 us -> none
    convert_element_type x2 -> x0, local copies, waits for them, and re-layouts: 7 us -> none  [the longest x1 4.04 us: conv_terms(): (weight[..., None] * spread).astype(jnp.bfloat16).reshape(-1, members)]
    concatenate x3 -> x0, other arithmetic: 5.26 us -> none  [the longest x2 4.33 us: extended(): block = jnp.concatenate([low, block, high], axis=dim)]
    convert_element_type x3 -> x0, other arithmetic: 4.85 us -> none  [the longest x1 2.05 us: conv_terms(): weight[..., None] * spread]
  transfers between devices with their start and end apart: 5 -> 0, of which waited for: 2 -> 0; matrix products, arithmetic and copies ran while one was open for 22% -> 0% of each run, Pallas kernels for 0% -> 0%
where the time goes in v1:
time: 44.2 us; the launch traced here: 43.5 us
  Pallas kernels  38.1 us (86%)
  local copies, waits for them, and re-layouts  5.35 us (12%)
    pallas_call x1, Pallas kernels, shards(): pl.pallas_call(functools.partial(gather_kernel, n_lat, n_lon), out_shape=...  33.1 us
    unnamed x15, local copies, waits for them, and re-layouts  5.35 us
    pallas_call x1, Pallas kernels, shards(): pl.pallas_call(analyse_kernel, out_shape=jax.ShapeDtypeStruct((1, 1, memb...  4.99 us

profile of v1, /device:TPU:0, one launch (start us, length us, event | category | flops | bytes accessed | tf_op | source)
XLA Modules:
  0.0 43.5 jit_solution(12292946056665969080)
XLA Ops:
  0.0 0.8 %copy.9.sat_targets = s32[1,16,2]{2,1,0:T(8,128)S(1)} copy(s32[1,16,2]{1,2,0:T(2,128)} %param.15) | data formatting | bytes 256 | tf_op args[7]
  0.8 0.0 copy-start.1
  0.8 1.0 %copy-done.1 = bf16[1,16,32,512]{3,2,1,0:T(8,128)(2,1)S(1)} copy-done((bf16[1,16,32,512]{3,2,1,0:T(8,128)(2,1)S(1)}, bf16[1,16,32,512]{3,2,1,0:T(8,128)(2,1)}, u32[]{:S(2)}) %copy-start.1) | copy-done | bytes 524312
  1.8 0.0 copy-start.2
  1.8 0.9 %copy-done.2 = bf16[1,1,128,512]{3,2,1,0:T(8,128)(2,1)S(1)} copy-done((bf16[1,1,128,512]{3,2,1,0:T(8,128)(2,1)S(1)}, bf16[1,1,128,512]{3,2,1,0:T(8,128)(2,1)}, u32[]{:S(2)}) %copy-start.2) | copy-done | bytes 131096
  2.7 0.0 copy-start.3
  2.7 0.7 %copy-done.3 = bf16[1,16,32]{2,1,0:T(8,128)(2,1)S(1)} copy-done((bf16[1,16,32]{2,1,0:T(8,128)(2,1)S(1)}, bf16[1,16,32]{2,1,0:T(8,128)(2,1)}, u32[]{:S(2)}) %copy-start.3) | copy-done | bytes 1048
  3.4 0.0 copy-start.4
  3.4 0.7 %copy-done.4 = bf16[1,1,128]{2,1,0:T(2,128)(2,1)S(1)} copy-done((bf16[1,1,128]{2,1,0:T(2,128)(2,1)S(1)}, bf16[1,1,128]{2,1,0:T(2,128)(2,1)}, u32[]{:S(2)}) %copy-start.4) | copy-done | bytes 280
  4.0 0.0 copy-start.5
  4.0 0.7 %copy-done.5 = s32[1,1,128]{2,1,0:T(1,128)S(1)} copy-done((s32[1,1,128]{2,1,0:T(1,128)S(1)}, s32[1,1,128]{2,1,0:T(1,128)}, u32[]{:S(2)}) %copy-start.5) | copy-done | bytes 536
  4.7 0.0 copy-start.6
  4.7 0.7 %copy-done.6 = s32[1,16]{1,0:T(1,128)S(1)} copy-done((s32[1,16]{1,0:T(1,128)S(1)}, s32[1,16]{1,0:T(1,128)}, u32[]{:S(2)}) %copy-start.6) | copy-done | bytes 88
  5.4 0.0 copy-start
  5.4 33.1 %gather_grams.1.packed = f32[272,512]{1,0:T(8,128)S(1)} custom-call(bf16[1,1,128,512]{3,2,1,0:T(8,128)(2,1)S(1)} %copy-done.2, bf16[1,1,128]{2,1,0:T(2,128)(2,1)S(1)} %copy-done.4, s32[1,1,128]{2,1,0:T(1,128)S(1)} %copy-done.5, bf16[1,16,32,512]{3,2,1,0:T(8,128)(2,1)S(1)} %copy-done.1, bf16[1,16,32]{2,1,0:T(8,128)(2,1)S(1)} %copy-done.3, ...), custom_call_target="tpu_custom_call" | custom-call | flops 2751463424 | bytes 1048576 | tf_op jit(solution)/shard_map/gather_grams/pallas_call | solution.py:400
  38.5 0.0 copy-done
  38.5 5.0 %analyse.1 = f32[1,1,512,1024]{3,2,1,0:T(8,128)} custom-call(f32[272,512]{1,0:T(8,128)S(1)} %gather_grams.1.packed, bf16[1,1,512,1024]{3,2,1,0:T(8,128)(2,1)S(1)} %copy-done), custom_call_target="tpu_custom_call" | custom-call | flops 1879048192 | bytes 3145728 | tf_op jit(solution)/shard_map/analyse/pallas_call | solution.py:429
Async XLA Ops:
  0.8 1.0 %copy-start.1 = (bf16[1,16,32,512]{3,2,1,0:T(8,128)(2,1)S(1)}, bf16[1,16,32,512]{3,2,1,0:T(8,128)(2,1)}, u32[]{:S(2)}) copy-start(bf16[1,16,32,512]{3,2,1,0:T(8,128)(2,1)} %sat_pert.1) | copy-start | bytes 1572868
  1.8 0.9 %copy-start.2 = (bf16[1,1,128,512]{3,2,1,0:T(8,128)(2,1)S(1)}, bf16[1,1,128,512]{3,2,1,0:T(8,128)(2,1)}, u32[]{:S(2)}) copy-start(bf16[1,1,128,512]{3,2,1,0:T(8,128)(2,1)} %conv_pert.1) | copy-start | bytes 393220
  2.7 0.7 %copy-start.3 = (bf16[1,16,32]{2,1,0:T(8,128)(2,1)S(1)}, bf16[1,16,32]{2,1,0:T(8,128)(2,1)}, u32[]{:S(2)}) copy-start(bf16[1,16,32]{2,1,0:T(8,128)(2,1)} %sat_misfit.1) | copy-start | bytes 3076
  3.4 0.7 %copy-start.4 = (bf16[1,1,128]{2,1,0:T(2,128)(2,1)S(1)}, bf16[1,1,128]{2,1,0:T(2,128)(2,1)}, u32[]{:S(2)}) copy-start(bf16[1,1,128]{2,1,0:T(2,128)(2,1)} %conv_misfit.1) | copy-start | bytes 772
  4.0 0.7 %copy-start.5 = (s32[1,1,128]{2,1,0:T(1,128)S(1)}, s32[1,1,128]{2,1,0:T(1,128)}, u32[]{:S(2)}) copy-start(s32[1,1,128]{2,1,0:T(1,128)} %conv_column.1) | copy-start | bytes 1540
  4.7 0.7 %copy-start.6 = (s32[1,16]{1,0:T(1,128)S(1)}, s32[1,16]{1,0:T(1,128)}, u32[]{:S(2)}) copy-start(s32[1,16]{1,0:T(1,128)} %sat_rows.1) | copy-start | bytes 196
  5.4 33.1 %copy-start = (bf16[1,1,512,1024]{3,2,1,0:T(8,128)(2,1)S(1)}, bf16[1,1,512,1024]{3,2,1,0:T(8,128)(2,1)}, u32[]{:S(2)}) copy-start(bf16[1,1,512,1024]{3,2,1,0:T(8,128)(2,1)} %background.1) | copy-start | bytes 3145732

commit v2 on v1

v2 whole, which is shorter than its diff:
```python
import functools

import jax
import jax.numpy as jnp
from jax import lax
from jax.experimental import pallas as pl
from jax.experimental.pallas import tpu as pltpu
from jax.sharding import PartitionSpec as P

BLK = 16
MESH = pl.DeviceIdType.MESH
F32 = jnp.float32
BF16 = jnp.bfloat16
EXTRA = 16
LANES = 128
STORES = 4


def dot(left, right):
    return lax.dot_general(left, right, (((1,), (0,)), ((), ())), preferred_element_type=F32)


def iota(shape, dim):
    return lax.broadcasted_iota(jnp.int32, shape, dim)


def gather_kernel(
    n_lat, n_lon,
    conv_pert, conv_misfit, conv_column, sat_pert, sat_misfit, sat_rows, sat_targets,
    out,
    small_misfit, small_column, tile_misfit, tile_rows, tile_targets,
    sat_buf, sat_lists, conv_buf, sat_flip, conv_flip, acc, send_buf, recv_buf,
    load, sat_send, sat_recv, conv_send, conv_recv, line_send, line_recv,
):
    chips = n_lon // 2
    band = lax.axis_index("lat")
    block = lax.axis_index("lon")
    chip, core = block // 2, block % 2
    sibling = 2 * chip + (1 - core)
    opposite = n_lon - 1 - block
    tiles, tile_obs = sat_misfit.shape[1], sat_misfit.shape[2]
    rows, members = tiles * tile_obs, sat_pert.shape[1]
    conv_obs = conv_pert.shape[2]
    half, lane_blocks = members // 2, members // LANES
    has_north, has_south = band > 0, band < n_lat - 1
    has_low, has_high = chip > 0, chip < chips - 1
    outer = jnp.logical_or(block == 0, block == n_lon - 1)
    mates = (
        (has_north, (band - 1, block)),
        (has_south, (band + 1, block)),
        (has_low, (band, block - 2)),
        (has_high, (band, block + 2)),
        (outer, (band, opposite)),
    )

    barrier = pltpu.get_barrier_semaphore()
    pl.semaphore_signal(barrier, inc=1, device_id=(band, sibling), device_id_type=MESH)
    for here, mate in mates:
        @pl.when(here)
        def _():
            pl.semaphore_signal(barrier, inc=1, device_id=mate, device_id_type=MESH)

    loads = [
        pltpu.make_async_copy(source, target, load.at[at])
        for at, (source, target) in enumerate(
            (
                (conv_pert.at[0, 0], conv_buf.at[0, 1, pl.ds(0, conv_obs)]),
                (conv_misfit, small_misfit),
                (conv_column, small_column),
                (sat_misfit, tile_misfit),
                (sat_rows, tile_rows),
                (sat_targets, tile_targets),
                (sat_pert, sat_buf.at[0]),
            )
        )
    ]
    for copy in loads:
        copy.start()
    pl.semaphore_wait(barrier, 1 + sum(here.astype(jnp.int32) for here, _ in mates))

    def sat_copy(source, target, at):
        return pltpu.make_async_remote_copy(
            src_ref=source, dst_ref=target, send_sem=sat_send.at[at], recv_sem=sat_recv.at[at],
            device_id=(band, sibling), device_id_type=MESH,
        )

    tile_copy = sat_copy(sat_pert, sat_buf.at[1], 0)
    list_copy = sat_copy(sat_lists.at[0], sat_lists.at[1], 1)
    tile_copy.start()

    for copy in loads[:6]:
        copy.wait()
    conv_buf[0, 1, conv_obs:, :] = jnp.concatenate(
        [
            jnp.broadcast_to(small_column[0].astype(F32).astype(BF16), (EXTRA, conv_obs)),
            jnp.broadcast_to(small_misfit[0], (EXTRA, conv_obs)),
            jnp.zeros((EXTRA, members - 2 * conv_obs), BF16),
        ],
        axis=1,
    )

    def conv_copy(group, slot, to_group, to_slot, sem, mate):
        return pltpu.make_async_remote_copy(
            src_ref=conv_buf.at[group, slot], dst_ref=conv_buf.at[to_group, to_slot],
            send_sem=conv_send.at[sem], recv_sem=conv_recv.at[sem],
            device_id=mate, device_id_type=MESH,
        )

    to_north = conv_copy(0, 1, 0, 2, 0, (band - 1, block))
    to_south = conv_copy(0, 1, 0, 0, 1, (band + 1, block))
    to_side = conv_copy(0, 1, 1, 1, 2, (band, sibling))
    relays = [conv_copy(0, 0, 1, 0, 3, (band, sibling)), conv_copy(0, 2, 1, 2, 4, (band, sibling))]
    around = conv_copy(0, 1, 2, 1, 5, (band, opposite))
    far_north = conv_copy(2, 1, 2, 2, 6, (band - 1, block))
    far_south = conv_copy(2, 1, 2, 0, 7, (band + 1, block))

    @pl.when(outer)
    def _():
        around.start()

    @pl.when(has_north)
    def _():
        to_north.start()

    @pl.when(has_south)
    def _():
        to_south.start()

    own_tile = iota((tiles, rows), 1) // tile_obs == iota((tiles, rows), 0)
    own_mask = own_tile.astype(BF16)
    spread_obs = (iota((tile_obs, rows), 1) % tile_obs == iota((tile_obs, rows), 0)).astype(BF16)
    misfit = jnp.sum(jnp.where(own_tile, dot(tile_misfit[0], spread_obs), 0.0), axis=0, keepdims=True)
    count = dot(jnp.broadcast_to(tile_rows[...].astype(F32).astype(BF16), (8, tiles)), own_mask)[0:1]
    live = (iota((1, rows), 1) % tile_obs).astype(F32) < count
    names = tile_targets[0].astype(F32)
    lists = [
        jnp.where(
            live,
            dot(jnp.broadcast_to(names[e : e + 1], (8, tiles)).astype(BF16), own_mask)[0:1],
            -1.0,
        )
        for e in range(2)
    ]
    place = iota((EXTRA, rows), 0)
    sat_lists[0] = jnp.where(
        place == 0, lists[0], jnp.where(place == 1, lists[1], jnp.where(place == 2, misfit, 0.0))
    ).astype(BF16)
    list_copy.start()
    to_side.start()

    blank = jnp.zeros((conv_obs + EXTRA, members), BF16)

    @pl.when(jnp.logical_not(has_north))
    def _():
        for group in range(3):
            conv_buf[group, 0] = blank

    @pl.when(jnp.logical_not(has_south))
    def _():
        for group in range(3):
            conv_buf[group, 2] = blank

    def flip_sat(side):
        sat_flip[:, pl.ds(side * rows, rows)] = sat_buf[side].T

    loads[6].wait()
    flip_sat(0)
    list_copy.wait_recv()
    tile_copy.wait_recv()
    flip_sat(1)

    def relay():
        @pl.when(has_north)
        def _():
            to_south.wait_recv()
            relays[0].start()

        @pl.when(has_south)
        def _():
            to_north.wait_recv()
            relays[1].start()

        @pl.when(outer)
        def _():
            around.wait_recv()

            @pl.when(has_north)
            def _():
                far_north.start()

            @pl.when(has_south)
            def _():
                far_south.start()

    def conv_ready():
        to_side.wait_recv()

        @pl.when(has_north)
        def _():
            relays[0].wait_recv()

        @pl.when(has_south)
        def _():
            relays[1].wait_recv()

        for group in range(2):
            for slot in range(3):
                at = (group * 3 + slot) * conv_obs
                conv_flip[:, at : at + conv_obs] = conv_buf[group, slot, :conv_obs, :].T

    def conv_weight(group, slot, target):
        column = conv_buf[group, slot, conv_obs:, :conv_obs][0:1].astype(F32)
        source = (block, sibling, opposite)[group]
        away = lax.rem(source - target + 1 + n_lon, n_lon) - 1
        row = jnp.floor(column * (1.0 / BLK))
        lat_place = BLK * (slot - 1.0) + row + 0.5 - 0.5 * BLK
        lon_place = BLK * away.astype(F32) + (column - BLK * row) + 0.5 - 0.5 * BLK
        weight = jnp.exp(-(lat_place * lat_place + lon_place * lon_place) / (2.0 * BLK * BLK))
        return jnp.where(away <= 1, weight, 0.0)

    place = iota((EXTRA, LANES), 0)
    eye = iota((half, half), 0) == iota((half, half), 1)
    upper = iota((half, half), 0) <= iota((half, half), 1)

    def add_terms(slot, scaled, spread, forced, first):
        top = dot(scaled[:half], spread)
        low = dot(scaled[half:], spread[:, half:])
        drive = dot(forced, spread)
        diagonal = jnp.sum(jnp.where(eye, low, 0.0), axis=0, keepdims=True)
        pieces = jnp.where(upper, top[:, :half], low), top[:, half:]
        tail = jnp.zeros((EXTRA, LANES), F32)
        for at in range(lane_blocks):
            lanes = slice(at * LANES, (at + 1) * LANES)
            tail += jnp.where(place == at, drive[0:1, lanes], 0.0)
            if at < lane_blocks // 2:
                tail += jnp.where(place == 2 * lane_blocks + at, diagonal[:, lanes], 0.0)
        for at in range(lane_blocks + 1):
            if at < lane_blocks:
                start = (at % (lane_blocks // 2)) * LANES
                term = pieces[at // (lane_blocks // 2)][:, start : start + LANES]
            else:
                term = tail
            into = slice(at * half, at * half + term.shape[0])
            if first:
                acc[slot, into, :] = term
            else:
                acc[slot, into, :] += term

    def add_conv(slot, target, groups):
        weights, pushes = [], []
        for group in groups:
            for side in range(3):
                weight = conv_weight(group, side, target)
                misfit = conv_buf[group, side, conv_obs:, conv_obs : 2 * conv_obs][0:1].astype(F32)
                weights.append(weight)
                pushes.append(weight * misfit)
        spreads = [conv_buf[group, side, :conv_obs, :] for group in groups for side in range(3)]
        flipped = conv_flip[...] if len(groups) == 2 else jnp.concatenate([each.T for each in spreads], axis=1)
        weight = jnp.concatenate(weights, axis=1)
        push = jnp.broadcast_to(jnp.concatenate(pushes, axis=1), (EXTRA, weight.shape[1]))
        scaled = (flipped.astype(F32) * weight).astype(BF16)
        add_terms(slot, scaled, jnp.concatenate(spreads, axis=0), push.astype(BF16), False)

    has_near = jnp.where(core == 0, chip < chips - 1, chip > 0)
    near = chip + 1 - 2 * core

    def compute(slot, to_chip):
        target = 2 * to_chip + core
        name = target.astype(F32)
        weights, pushes = [], []
        for side in range(2):
            lists = sat_lists[side].astype(F32)
            weight = jnp.where(lists[0:1] == name, 1.0, 0.0) + jnp.where(lists[1:2] == name, 0.5, 0.0)
            weights.append(weight)
            pushes.append(weight * lists[2:3])
        weight = jnp.concatenate(weights, axis=1)
        push = jnp.concatenate(pushes, axis=1)
        scaled = sat_flip[...] * weight.astype(BF16)
        spread = sat_buf[...].reshape(2 * rows, members)
        add_terms(slot, scaled, spread, jnp.broadcast_to(push, (EXTRA, 2 * rows)).astype(BF16), True)

        @pl.when(jnp.logical_or(to_chip == chip, to_chip == near))
        def _():
            add_conv(slot, target, (0, 1))

    def line_copy(way, to_chip):
        ahead = block + 2 if way == 0 else block - 2
        return pltpu.make_async_remote_copy(
            src_ref=send_buf.at[way, to_chip], dst_ref=recv_buf.at[way, to_chip],
            send_sem=line_send.at[way, to_chip], recv_sem=line_recv.at[way, to_chip],
            device_id=(band, ahead), device_id_type=MESH,
        )

    def step_of(way, step):
        if way == 0:
            to_chip = chips - 1 + chip - step
            return to_chip, jnp.logical_and(to_chip > chip, to_chip < chips), has_low
        to_chip = step + chip - chips + 1
        return to_chip, jnp.logical_and(to_chip >= 0, to_chip < chip), has_high

    def finish(way, slot, to_chip, behind):
        @pl.when(behind)
        def _():
            line_copy(way, to_chip).wait_recv()
            acc[slot] += recv_buf[way, to_chip].astype(F32)

        tail = acc[slot, lane_blocks * half :, :]
        parts = [tail[at * lane_blocks : (at + 1) * lane_blocks] for at in range(4)]
        high, kept = (parts[at].astype(BF16).astype(F32) for at in (0, 2))
        send_buf[way, to_chip, : lane_blocks * half, :] = acc[slot, : lane_blocks * half, :].astype(BF16)
        send_buf[way, to_chip, lane_blocks * half :, :] = jnp.concatenate(
            [high, parts[0] + parts[1] - high, kept, parts[2] + parts[3] - kept], axis=0
        ).astype(BF16)
        line_copy(way, to_chip).start()

    def step_body(step, carry):
        for way in range(2):
            to_chip, wanted, behind = step_of(way, step)

            @pl.when(wanted)
            def _():
                @pl.when(to_chip == near)
                def _():
                    conv_ready()

                compute(way, to_chip)
        for way in range(2):
            to_chip, wanted, behind = step_of(way, step)

            @pl.when(wanted)
            def _():
                finish(way, way, to_chip, behind)

        if chips > 2:
            @pl.when(step == 0)
            def _():
                relay()

        return carry

    if chips == 2:
        relay()

    lax.fori_loop(0, chips - 1, step_body, 0)

    @pl.when(jnp.logical_not(has_near))
    def _():
        conv_ready()

    compute(0, chip)

    @pl.when(outer)
    def _():
        @pl.when(has_north)
        def _():
            far_south.wait_recv()

        @pl.when(has_south)
        def _():
            far_north.wait_recv()

        add_conv(0, block, (2,))

    @pl.when(has_low)
    def _():
        line_copy(0, chip).wait_recv()
        acc[0] += recv_buf[0, chip].astype(F32)

    @pl.when(has_high)
    def _():
        line_copy(1, chip).wait_recv()
        acc[0] += recv_buf[1, chip].astype(F32)

    out[...] = acc[0]

    tile_copy.wait_send()
    list_copy.wait_send()
    to_side.wait_send()

    @pl.when(outer)
    def _():
        around.wait_send()

        @pl.when(has_north)
        def _():
            far_north.wait_send()

        @pl.when(has_south)
        def _():
            far_south.wait_send()

    @pl.when(has_north)
    def _():
        to_north.wait_send()
        relays[0].wait_send()

    @pl.when(has_south)
    def _():
        to_south.wait_send()
        relays[1].wait_send()

    def drain(step, carry):
        for way in range(2):
            to_chip, wanted, _ = step_of(way, step)

            @pl.when(wanted)
            def _():
                line_copy(way, to_chip).wait_send()
        return carry

    lax.fori_loop(0, chips - 1, drain, 0)


def analyse_kernel(packed, background, out, members_buf, out_buf, load, store):
    members = background.shape[2]
    fetch = pltpu.make_async_copy(background.at[0, 0], members_buf, load)
    fetch.start()
    half, lane_blocks = members // 2, members // LANES
    blocks = [packed[at * half : (at + 1) * half] for at in range(lane_blocks)]
    field = jnp.concatenate(blocks[: lane_blocks // 2], axis=1)
    cross = jnp.concatenate(blocks[lane_blocks // 2 :], axis=1)
    tail = packed[lane_blocks * half :]

    def tail_row(first, count):
        at = [first * lane_blocks + each for each in range(count)]
        return jnp.concatenate(
            [tail[each : each + 1] + tail[each + lane_blocks : each + lane_blocks + 1] for each in at], axis=1
        )

    drive = tail_row(0, lane_blocks)
    diagonal = tail_row(2, lane_blocks // 2)
    row, col = iota((half, half), 0), iota((half, half), 1)
    strict = jnp.where(row < col, field, 0.0)
    under = jnp.where(row > col, field, 0.0)
    first = jnp.where(row <= col, field, 0.0) + strict.T
    second = under + under.T + jnp.where(row == col, diagonal, 0.0)
    gram = jnp.concatenate(
        [jnp.concatenate([first, cross], axis=1), jnp.concatenate([cross.T, second], axis=1)], axis=0
    )
    one = (iota((members, members), 0) == iota((members, members), 1)).astype(F32)
    system = (members - 1.0) * one + gram
    scale = jnp.sqrt(jnp.sum(jnp.sum(system * system, axis=0, keepdims=True), axis=1, keepdims=True))
    y = system / scale
    yb = y.astype(BF16)
    square = dot(yb, yb)
    u = 1.5 * y - 0.5 * square
    w = 0.25 * square - 1.5 * y
    q = 2.25 * u + dot(u.astype(BF16), w.astype(BF16))
    e2 = -0.75 * y - 0.5 * q
    e2b = e2.astype(BF16)
    f = 2.25 * y + dot(yb, e2b)
    h = 4.5 * e2 + dot(e2b, e2b)
    e3 = 1.5 * e2 - 0.5 * (5.0625 * f + dot(f.astype(BF16), h.astype(BF16)))
    e3b = e3.astype(BF16)

    def times_root(vector):
        high = vector.astype(BF16)
        low = (vector - high.astype(F32)).astype(BF16)
        place = iota((16, members), 0)
        both = jnp.where(place == 0, high.astype(F32), jnp.where(place == 1, low.astype(F32), 0.0))
        product = dot(both.astype(BF16), e3b)
        return 3.375 * vector + product[0:1] + product[1:2]

    mean_weight = times_root(times_root(drive)) / scale
    transform = (jnp.sqrt((members - 1.0) / scale) * (3.375 * one + e3)).astype(BF16)

    fetch.wait()
    ensemble = members_buf[...].astype(F32)
    state_mean = jnp.mean(ensemble, axis=0, keepdims=True)
    anomaly = (ensemble - state_mean).astype(BF16)
    high = mean_weight.astype(BF16)
    low = (mean_weight - high.astype(F32)).astype(BF16)
    place = iota((16, members), 0)
    both = jnp.where(place == 0, high.astype(F32), jnp.where(place == 1, low.astype(F32), 0.0))
    shift = dot(both.astype(BF16), anomaly)
    centre = state_mean + shift[0:1] + shift[1:2]
    part = members // STORES
    stores = [
        pltpu.make_async_copy(
            out_buf.at[pl.ds(at * part, part)], out.at[0, 0, pl.ds(at * part, part)], store.at[at]
        )
        for at in range(STORES)
    ]
    for at, copy in enumerate(stores):
        out_buf[at * part : (at + 1) * part, :] = dot(transform[at * part : (at + 1) * part], anomaly) + centre
        copy.start()
    for copy in stores:
        copy.wait()


def shards(
    n_lat, n_lon,
    background, conv_pert, conv_misfit, conv_column, sat_pert, sat_misfit, sat_rows, sat_targets,
):
    members, cells = background.shape[2:]
    tiles, tile_obs = sat_pert.shape[1:3]
    conv_obs = conv_pert.shape[2]
    rows, chips, half = tiles * tile_obs, n_lon // 2, members // 2
    vmem = pl.BlockSpec(memory_space=pltpu.VMEM)
    lanes_long = members // LANES * half + EXTRA
    hbm = pl.BlockSpec(memory_space=pltpu.HBM)
    packed = pl.pallas_call(
        functools.partial(gather_kernel, n_lat, n_lon),
        out_shape=jax.ShapeDtypeStruct((lanes_long, LANES), F32),
        in_specs=[hbm] * 7,
        out_specs=vmem,
        scratch_shapes=[
            pltpu.VMEM((1, 1, conv_obs), BF16),
            pltpu.VMEM((1, 1, conv_obs), jnp.int32),
            pltpu.VMEM((1, tiles, tile_obs), BF16),
            pltpu.VMEM((1, tiles), jnp.int32),
            pltpu.VMEM((1, 2, tiles), jnp.int32),
            pltpu.VMEM((2, rows, members), BF16),
            pltpu.VMEM((2, EXTRA, rows), BF16),
            pltpu.VMEM((3, 3, conv_obs + EXTRA, members), BF16),
            pltpu.VMEM((members, 2 * rows), BF16),
            pltpu.VMEM((members, 6 * conv_obs), BF16),
            pltpu.VMEM((2, lanes_long, LANES), F32),
            pltpu.VMEM((2, chips, lanes_long, LANES), BF16),
            pltpu.VMEM((2, chips, lanes_long, LANES), BF16),
            pltpu.SemaphoreType.DMA((7,)),
            pltpu.SemaphoreType.DMA((2,)),
            pltpu.SemaphoreType.DMA((2,)),
            pltpu.SemaphoreType.DMA((8,)),
            pltpu.SemaphoreType.DMA((8,)),
            pltpu.SemaphoreType.DMA((2, chips)),
            pltpu.SemaphoreType.DMA((2, chips)),
        ],
        compiler_params=pltpu.CompilerParams(
            collective_id=0, has_side_effects=True, vmem_limit_bytes=64 * 1024 * 1024
        ),
        cost_estimate=pl.CostEstimate(
            flops=2 * (chips * 2 * rows + 9 * conv_obs) * members * members,
            bytes_accessed=4 * rows * members, transcendentals=0,
        ),
        name="gather_grams",
    )(
        conv_pert, conv_misfit, conv_column, sat_pert.reshape(rows, members), sat_misfit, sat_rows,
        jnp.swapaxes(sat_targets, 1, 2),
    )
    return pl.pallas_call(
        analyse_kernel,
        out_shape=jax.ShapeDtypeStruct((1, 1, members, cells), F32),
        in_specs=[vmem, hbm],
        out_specs=hbm,
        scratch_shapes=[
            pltpu.VMEM((members, cells), BF16),
            pltpu.VMEM((members, cells), F32),
            pltpu.SemaphoreType.DMA,
            pltpu.SemaphoreType.DMA((STORES,)),
        ],
        compiler_params=pltpu.CompilerParams(vmem_limit_bytes=64 * 1024 * 1024),
        cost_estimate=pl.CostEstimate(
            flops=14 * members * members * members, bytes_accessed=6 * members * cells, transcendentals=0
        ),
        name="analyse",
    )(packed, background)


def solution(mesh):
    placed = (
        P("lat", "lon", None, None),
        P("lat", "lon", None, None),
        P("lat", "lon", None),
        P("lat", "lon", None),
        P("lat", "lon", None, None),
        P("lat", "lon", None),
        P("lat", "lon"),
        P("lat", "lon", None),
    )
    return jax.shard_map(
        functools.partial(shards, mesh.shape["lat"], mesh.shape["lon"]),
        mesh=mesh, in_specs=placed, out_specs=P("lat", "lon", None, None), check_vma=False,
    )
```

time: 44.2 us -> 38 us (0.86); the launches traced: 43.5 us -> 37.9 us
  local copies, waits for them, and re-layouts: 5.35 us -> 0 us
    unnamed x15 -> x0, local copies, waits for them, and re-layouts: 5.35 us -> none
    pallas_call x1, Pallas kernels: 33.1 us -> 32.1 us  [shards(): pl.pallas_call(functools.partial(gather_kernel, n_lat, n_lon), out_shape=...]
    pallas_call x1, Pallas kernels: 4.99 us -> 5.78 us  [shards(): pl.pallas_call(analyse_kernel, out_shape=jax.ShapeDtypeStruct((1, 1, memb...]
where the time goes in v2:
time: 38 us; the launch traced here: 37.9 us
  Pallas kernels  37.8 us (99%)
    pallas_call x1, Pallas kernels, shards(): pl.pallas_call(functools.partial(gather_kernel, n_lat, n_lon), out_shape=...  32.1 us
    pallas_call x1, Pallas kernels, shards(): pl.pallas_call(analyse_kernel, out_shape=jax.ShapeDtypeStruct((1, 1, memb...  5.78 us

profile of v2, /device:TPU:0, one launch (start us, length us, event | category | flops | bytes accessed | tf_op | source)
XLA Modules:
  0.0 37.9 jit_solution(13286825326100294202)
XLA Ops:
  0.0 32.1 %gather_grams.1.packed = f32[1040,128]{1,0:T(8,128)} custom-call(bf16[1,1,128,512]{3,2,1,0:T(8,128)(2,1)} %conv_pert.1, bf16[1,1,128]{2,1,0:T(2,128)(2,1)} %conv_misfit.1, s32[1,1,128]{2,1,0:T(1,128)} %conv_column.1, bf16[512,512]{1,0:T(8,128)(2,1)} %bitcast.2, bf16[1,16,32]{2,1,0:T(8,128)(2,1)} %sat_misfit.1, s32[1,16]{1,0:T(1,128)} %sat_rows.1, ...), custom_call_target="tpu_custom_call" | custom-call | flops 2751463424 | bytes 1048576 | tf_op jit(solution)/shard_map/gather_grams/pallas_call | solution.py:502
  32.1 5.8 %analyse.1 = f32[1,1,512,1024]{3,2,1,0:T(8,128)} custom-call(f32[1040,128]{1,0:T(8,128)} %gather_grams.1.packed, bf16[1,1,512,1024]{3,2,1,0:T(8,128)(2,1)} %background.1), custom_call_target="tpu_custom_call" | custom-call | flops 1879048192 | bytes 3145728 | tf_op jit(solution)/shard_map/analyse/pallas_call | solution.py:541

commit v3 on v2

--- a/solution.py
+++ b/solution.py
@@ -26,9 +26,9 @@
 
 def gather_kernel(
     n_lat, n_lon,
-    conv_pert, conv_misfit, conv_column, sat_pert, sat_misfit, sat_rows, sat_targets,
-    out,
-    small_misfit, small_column, tile_misfit, tile_rows, tile_targets,
+    background, conv_pert, conv_misfit, conv_column, sat_pert, sat_misfit, sat_rows, sat_targets,
+    out, anomaly, centre,
+    members_buf, anomaly_buf, small_misfit, small_column, tile_misfit, tile_rows, tile_targets,
     sat_buf, sat_lists, conv_buf, sat_flip, conv_flip, acc, send_buf, recv_buf,
     load, sat_send, sat_recv, conv_send, conv_recv, line_send, line_recv,
 ):
@@ -71,6 +71,7 @@
                 (sat_rows, tile_rows),
                 (sat_targets, tile_targets),
                 (sat_pert, sat_buf.at[0]),
+                (background.at[0, 0], members_buf),
             )
         )
     ]
@@ -161,13 +162,7 @@
             conv_buf[group, 2] = blank
 
     def flip_sat(side):
-        sat_flip[:, pl.ds(side * rows, rows)] = sat_buf[side].T
-
-    loads[6].wait()
-    flip_sat(0)
-    list_copy.wait_recv()
-    tile_copy.wait_recv()
-    flip_sat(1)
+        sat_flip[side] = sat_buf[side].T
 
     def relay():
         @pl.when(has_north)
@@ -222,31 +217,39 @@
     eye = iota((half, half), 0) == iota((half, half), 1)
     upper = iota((half, half), 0) <= iota((half, half), 1)
 
-    def add_terms(slot, scaled, spread, forced, first):
-        top = dot(scaled[:half], spread)
-        low = dot(scaled[half:], spread[:, half:])
-        drive = dot(forced, spread)
-        diagonal = jnp.sum(jnp.where(eye, low, 0.0), axis=0, keepdims=True)
-        pieces = jnp.where(upper, top[:, :half], low), top[:, half:]
-        tail = jnp.zeros((EXTRA, LANES), F32)
-        for at in range(lane_blocks):
-            lanes = slice(at * LANES, (at + 1) * LANES)
-            tail += jnp.where(place == at, drive[0:1, lanes], 0.0)
-            if at < lane_blocks // 2:
-                tail += jnp.where(place == 2 * lane_blocks + at, diagonal[:, lanes], 0.0)
-        for at in range(lane_blocks + 1):
-            if at < lane_blocks:
-                start = (at % (lane_blocks // 2)) * LANES
-                term = pieces[at // (lane_blocks // 2)][:, start : start + LANES]
-            else:
-                term = tail
-            into = slice(at * half, at * half + term.shape[0])
+    cut = lane_blocks // 2 * half
+    parts = (slice(0, cut), slice(cut, 2 * cut + EXTRA))
+
+    def add_terms(slot, part, flipped, weight, push, spread, first):
+        def put(into, term):
             if first:
                 acc[slot, into, :] = term
             else:
                 acc[slot, into, :] += term
 
-    def add_conv(slot, target, groups):
+        def scaled(rows_of):
+            if weight.dtype == BF16:
+                return rows_of * weight
+            return (rows_of.astype(F32) * weight).astype(BF16)
+
+        if part == 0:
+            piece = dot(scaled(flipped[:half]), spread[:, half:])
+        else:
+            low = dot(scaled(flipped[half:]), spread[:, half:])
+            piece = jnp.where(upper, dot(scaled(flipped[:half]), spread[:, :half]), low)
+            drive = dot(jnp.broadcast_to(push, (EXTRA, push.shape[1])).astype(BF16), spread)
+            diagonal = jnp.sum(jnp.where(eye, low, 0.0), axis=0, keepdims=True)
+            tail = jnp.zeros((EXTRA, LANES), F32)
+            for at in range(lane_blocks):
+                lanes = slice(at * LANES, (at + 1) * LANES)
+                tail += jnp.where(place == at, drive[0:1, lanes], 0.0)
+                if at < lane_blocks // 2:
+                    tail += jnp.where(place == 2 * lane_blocks + at, diagonal[:, lanes], 0.0)
+            put(slice(2 * cut, 2 * cut + EXTRA), tail)
+        for at in range(lane_blocks // 2):
+            put(slice(part * cut + at * half, part * cut + (at + 1) * half), piece[:, at * LANES : (at + 1) * LANES])
+
+    def add_conv(slot, part, target, groups):
         weights, pushes = [], []
         for group in groups:
             for side in range(3):
@@ -256,38 +259,26 @@
                 pushes.append(weight * misfit)
         spreads = [conv_buf[group, side, :conv_obs, :] for group in groups for side in range(3)]
         flipped = conv_flip[...] if len(groups) == 2 else jnp.concatenate([each.T for each in spreads], axis=1)
-        weight = jnp.concatenate(weights, axis=1)
-        push = jnp.broadcast_to(jnp.concatenate(pushes, axis=1), (EXTRA, weight.shape[1]))
-        scaled = (flipped.astype(F32) * weight).astype(BF16)
-        add_terms(slot, scaled, jnp.concatenate(spreads, axis=0), push.astype(BF16), False)
+        weight, push = (jnp.concatenate(each, axis=1) for each in (weights, pushes))
+        add_terms(slot, part, flipped, weight, push, jnp.concatenate(spreads, axis=0), False)
+
+    def add_sat(slot, part, to_chip, side):
+        name = (2 * to_chip + core).astype(F32)
+        lists = sat_lists[side].astype(F32)
+        weight = jnp.where(lists[0:1] == name, 1.0, 0.0) + jnp.where(lists[1:2] == name, 0.5, 0.0)
+        add_terms(
+            slot, part, sat_flip[side], weight.astype(BF16), weight * lists[2:3], sat_buf[side], side == 0
+        )
 
     has_near = jnp.where(core == 0, chip < chips - 1, chip > 0)
     near = chip + 1 - 2 * core
 
-    def compute(slot, to_chip):
-        target = 2 * to_chip + core
-        name = target.astype(F32)
-        weights, pushes = [], []
-        for side in range(2):
-            lists = sat_lists[side].astype(F32)
-            weight = jnp.where(lists[0:1] == name, 1.0, 0.0) + jnp.where(lists[1:2] == name, 0.5, 0.0)
-            weights.append(weight)
-            pushes.append(weight * lists[2:3])
-        weight = jnp.concatenate(weights, axis=1)
-        push = jnp.concatenate(pushes, axis=1)
-        scaled = sat_flip[...] * weight.astype(BF16)
-        spread = sat_buf[...].reshape(2 * rows, members)
-        add_terms(slot, scaled, spread, jnp.broadcast_to(push, (EXTRA, 2 * rows)).astype(BF16), True)
-
-        @pl.when(jnp.logical_or(to_chip == chip, to_chip == near))
-        def _():
-            add_conv(slot, target, (0, 1))
-
-    def line_copy(way, to_chip):
+    def line_copy(way, to_chip, part):
         ahead = block + 2 if way == 0 else block - 2
+        span = pl.ds(parts[part].start, parts[part].stop - parts[part].start)
         return pltpu.make_async_remote_copy(
-            src_ref=send_buf.at[way, to_chip], dst_ref=recv_buf.at[way, to_chip],
-            send_sem=line_send.at[way, to_chip], recv_sem=line_recv.at[way, to_chip],
+            src_ref=send_buf.at[way, to_chip, span], dst_ref=recv_buf.at[way, to_chip, span],
+            send_sem=line_send.at[way, to_chip, part], recv_sem=line_recv.at[way, to_chip, part],
             device_id=(band, ahead), device_id_type=MESH,
         )
 
@@ -298,38 +289,63 @@
         to_chip = step + chip - chips + 1
         return to_chip, jnp.logical_and(to_chip >= 0, to_chip < chip), has_high
 
-    def finish(way, slot, to_chip, behind):
+    def finish(way, to_chip, behind, part):
         @pl.when(behind)
         def _():
-            line_copy(way, to_chip).wait_recv()
-            acc[slot] += recv_buf[way, to_chip].astype(F32)
-
-        tail = acc[slot, lane_blocks * half :, :]
-        parts = [tail[at * lane_blocks : (at + 1) * lane_blocks] for at in range(4)]
-        high, kept = (parts[at].astype(BF16).astype(F32) for at in (0, 2))
-        send_buf[way, to_chip, : lane_blocks * half, :] = acc[slot, : lane_blocks * half, :].astype(BF16)
-        send_buf[way, to_chip, lane_blocks * half :, :] = jnp.concatenate(
-            [high, parts[0] + parts[1] - high, kept, parts[2] + parts[3] - kept], axis=0
-        ).astype(BF16)
-        line_copy(way, to_chip).start()
+            line_copy(way, to_chip, part).wait_recv()
+            acc[way, parts[part], :] += recv_buf[way, to_chip, parts[part], :].astype(F32)
+
+        send_buf[way, to_chip, part * cut : (part + 1) * cut, :] = acc[
+            way, part * cut : (part + 1) * cut, :
+        ].astype(BF16)
+        if part == 1:
+            tail = acc[way, 2 * cut :, :]
+            four = [tail[at * lane_blocks : (at + 1) * lane_blocks] for at in range(4)]
+            high, kept = (four[at].astype(BF16).astype(F32) for at in (0, 2))
+            send_buf[way, to_chip, 2 * cut :, :] = jnp.concatenate(
+                [high, four[0] + four[1] - high, kept, four[2] + four[3] - kept], axis=0
+            ).astype(BF16)
+        line_copy(way, to_chip, part).start()
+
+    loads[6].wait()
+    flip_sat(0)
+    for way in range(2):
+        to_chip, wanted, _ = step_of(way, 0)
+
+        @pl.when(wanted)
+        def _():
+            for part in range(2):
+                add_sat(way, part, to_chip, 0)
+
+    list_copy.wait_recv()
+    tile_copy.wait_recv()
+    flip_sat(1)
 
     def step_body(step, carry):
-        for way in range(2):
-            to_chip, wanted, behind = step_of(way, step)
-
-            @pl.when(wanted)
-            def _():
-                @pl.when(to_chip == near)
+        for part in range(2):
+            for way in range(2):
+                to_chip, wanted, behind = step_of(way, step)
+
+                @pl.when(wanted)
                 def _():
-                    conv_ready()
-
-                compute(way, to_chip)
-        for way in range(2):
-            to_chip, wanted, behind = step_of(way, step)
-
-            @pl.when(wanted)
-            def _():
-                finish(way, way, to_chip, behind)
+                    @pl.when(step > 0)
+                    def _():
+                        add_sat(way, part, to_chip, 0)
+
+                    add_sat(way, part, to_chip, 1)
+
+                    @pl.when(to_chip == near)
+                    def _():
+                        if part == 0:
+                            conv_ready()
+                        add_conv(way, part, 2 * to_chip + core, (0, 1))
+
+            for way in range(2):
+                to_chip, wanted, behind = step_of(way, step)
+
+                @pl.when(wanted)
+                def _():
+                    finish(way, to_chip, behind, part)
 
         if chips > 2:
             @pl.when(step == 0)
@@ -347,7 +363,10 @@
     def _():
         conv_ready()
 
-    compute(0, chip)
+    for part in range(2):
+        for side in range(2):
+            add_sat(0, part, chip, side)
+        add_conv(0, part, block, (0, 1))
 
     @pl.when(outer)
     def _():
@@ -359,20 +378,27 @@
         def _():
             far_north.wait_recv()
 
-        add_conv(0, block, (2,))
-
-    @pl.when(has_low)
-    def _():
-        line_copy(0, chip).wait_recv()
-        acc[0] += recv_buf[0, chip].astype(F32)
-
-    @pl.when(has_high)
-    def _():
-        line_copy(1, chip).wait_recv()
-        acc[0] += recv_buf[1, chip].astype(F32)
-
-    out[...] = acc[0]
-
+        for part in range(2):
+            add_conv(0, part, block, (2,))
+
+    loads[7].wait()
+    ensemble = members_buf[...].astype(F32)
+    state_mean = jnp.mean(ensemble, axis=0, keepdims=True)
+    anomaly_buf[...] = (ensemble - state_mean).astype(BF16)
+    keep = pltpu.make_async_copy(anomaly_buf, anomaly, load.at[8])
+    keep.start()
+    centre[...] = jnp.broadcast_to(state_mean, centre.shape)
+
+    for part in range(2):
+        for way, behind in enumerate((has_low, has_high)):
+            @pl.when(behind)
+            def _():
+                line_copy(way, chip, part).wait_recv()
+                acc[0, parts[part], :] += recv_buf[way, chip, parts[part], :].astype(F32)
+
+        out[parts[part], :] = acc[0, parts[part], :]
+
+    keep.wait()
     tile_copy.wait_send()
     list_copy.wait_send()
     to_side.wait_send()
@@ -405,20 +431,21 @@
 
             @pl.when(wanted)
             def _():
-                line_copy(way, to_chip).wait_send()
+                for part in range(2):
+                    line_copy(way, to_chip, part).wait_send()
         return carry
 
     lax.fori_loop(0, chips - 1, drain, 0)
 
 
-def analyse_kernel(packed, background, out, members_buf, out_buf, load, store):
-    members = background.shape[2]
-    fetch = pltpu.make_async_copy(background.at[0, 0], members_buf, load)
+def analyse_kernel(packed, state_mean, spread, out, anomaly_buf, out_buf, load, store):
+    members = spread.shape[0]
+    fetch = pltpu.make_async_copy(spread, anomaly_buf, load)
     fetch.start()
     half, lane_blocks = members // 2, members // LANES
     blocks = [packed[at * half : (at + 1) * half] for at in range(lane_blocks)]
-    field = jnp.concatenate(blocks[: lane_blocks // 2], axis=1)
-    cross = jnp.concatenate(blocks[lane_blocks // 2 :], axis=1)
+    cross = jnp.concatenate(blocks[: lane_blocks // 2], axis=1)
+    field = jnp.concatenate(blocks[lane_blocks // 2 :], axis=1)
     tail = packed[lane_blocks * half :]
 
     def tail_row(first, count):
@@ -465,15 +492,13 @@
     transform = (jnp.sqrt((members - 1.0) / scale) * (3.375 * one + e3)).astype(BF16)
 
     fetch.wait()
-    ensemble = members_buf[...].astype(F32)
-    state_mean = jnp.mean(ensemble, axis=0, keepdims=True)
-    anomaly = (ensemble - state_mean).astype(BF16)
+    anomaly = anomaly_buf[...]
     high = mean_weight.astype(BF16)
     low = (mean_weight - high.astype(F32)).astype(BF16)
     place = iota((16, members), 0)
     both = jnp.where(place == 0, high.astype(F32), jnp.where(place == 1, low.astype(F32), 0.0))
     shift = dot(both.astype(BF16), anomaly)
-    centre = state_mean + shift[0:1] + shift[1:2]
+    centre = state_mean[0:1] + shift[0:1] + shift[1:2]
     part = members // STORES
     stores = [
         pltpu.make_async_copy(
@@ -499,12 +524,18 @@
     vmem = pl.BlockSpec(memory_space=pltpu.VMEM)
     lanes_long = members // LANES * half + EXTRA
     hbm = pl.BlockSpec(memory_space=pltpu.HBM)
-    packed = pl.pallas_call(
+    packed, anomaly, state_mean = pl.pallas_call(
         functools.partial(gather_kernel, n_lat, n_lon),
-        out_shape=jax.ShapeDtypeStruct((lanes_long, LANES), F32),
-        in_specs=[hbm] * 7,
-        out_specs=vmem,
+        out_shape=(
+            jax.ShapeDtypeStruct((lanes_long, LANES), F32),
+            jax.ShapeDtypeStruct((members, cells), BF16),
+            jax.ShapeDtypeStruct((8, cells), F32),
+        ),
+        in_specs=[hbm] * 8,
+        out_specs=(vmem, hbm, vmem),
         scratch_shapes=[
+            pltpu.VMEM((members, cells), BF16),
+            pltpu.VMEM((members, cells), BF16),
             pltpu.VMEM((1, 1, conv_obs), BF16),
             pltpu.VMEM((1, 1, conv_obs), jnp.int32),
             pltpu.VMEM((1, tiles, tile_obs), BF16),
@@ -513,18 +544,18 @@
             pltpu.VMEM((2, rows, members), BF16),
             pltpu.VMEM((2, EXTRA, rows), BF16),
             pltpu.VMEM((3, 3, conv_obs + EXTRA, members), BF16),
-            pltpu.VMEM((members, 2 * rows), BF16),
+            pltpu.VMEM((2, members, rows), BF16),
             pltpu.VMEM((members, 6 * conv_obs), BF16),
             pltpu.VMEM((2, lanes_long, LANES), F32),
             pltpu.VMEM((2, chips, lanes_long, LANES), BF16),
             pltpu.VMEM((2, chips, lanes_long, LANES), BF16),
-            pltpu.SemaphoreType.DMA((7,)),
+            pltpu.SemaphoreType.DMA((9,)),
             pltpu.SemaphoreType.DMA((2,)),
             pltpu.SemaphoreType.DMA((2,)),
             pltpu.SemaphoreType.DMA((8,)),
             pltpu.SemaphoreType.DMA((8,)),
-            pltpu.SemaphoreType.DMA((2, chips)),
-            pltpu.SemaphoreType.DMA((2, chips)),
+            pltpu.SemaphoreType.DMA((2, chips, 2)),
+            pltpu.SemaphoreType.DMA((2, chips, 2)),
         ],
         compiler_params=pltpu.CompilerParams(
             collective_id=0, has_side_effects=True, vmem_limit_bytes=64 * 1024 * 1024
@@ -535,13 +566,13 @@
         ),
         name="gather_grams",
     )(
-        conv_pert, conv_misfit, conv_column, sat_pert.reshape(rows, members), sat_misfit, sat_rows,
+        background, conv_pert, conv_misfit, conv_column, sat_pert.reshape(rows, members), sat_misfit, sat_rows,
         jnp.swapaxes(sat_targets, 1, 2),
     )
     return pl.pallas_call(
         analyse_kernel,
         out_shape=jax.ShapeDtypeStruct((1, 1, members, cells), F32),
-        in_specs=[vmem, hbm],
+        in_specs=[vmem, vmem, hbm],
         out_specs=hbm,
         scratch_shapes=[
             pltpu.VMEM((members, cells), BF16),
@@ -554,7 +585,7 @@
             flops=14 * members * members * members, bytes_accessed=6 * members * cells, transcendentals=0
         ),
         name="analyse",
-    )(packed, background)
+    )(packed, state_mean, anomaly)
 
 
 def solution(mesh):

time: 38 us -> 32.3 us (0.85)
  Pallas kernels: 37.8 us -> 32.1 us
    pallas_call x1, Pallas kernels: 32.1 us -> 26.6 us  [shards(): pl.pallas_call(functools.partial(gather_kernel, n_lat, n_lon), out_shape=...]
where the time goes in v3:
time: 32.3 us; the launch traced here: 32.1 us
  Pallas kernels  32.1 us (99%)
    pallas_call x1, Pallas kernels, shards(): pl.pallas_call(functools.partial(gather_kernel, n_lat, n_lon), out_shape=...  26.6 us
    pallas_call x1, Pallas kernels, shards(): pl.pallas_call(analyse_kernel, out_shape=jax.ShapeDtypeStruct((1, 1, memb...  5.55 us

profile of v3, /device:TPU:0, one launch (start us, length us, event | category | flops | bytes accessed | tf_op | source)
XLA Modules:
  0.0 32.1 jit_solution(8082796829367838268)
XLA Ops:
  0.0 26.6 %gather_grams.1 = (f32[1040,128]{1,0:T(8,128)}, bf16[512,1024]{1,0:T(8,128)(2,1)}, f32[8,1024]{1,0:T(8,128)}) custom-call(bf16[1,1,512,1024]{3,2,1,0:T(8,128)(2,1)} %background.1, bf16[1,1,128,512]{3,2,1,0:T(8,128)(2,1)} %conv_pert.1, bf16[1,1,128]{2,1,0:T(2,128)(2,1)} %conv_misfit.1, s32[1,1,128]{2,1,0:T(1,128)} %conv_column.1, bf16[512,512]{1,0:T(8,128)(2,1)} %bitcast.2, ...), custom_call_target="tpu_custom_call" | custom-call | flops 2751463424 | bytes 1048576 | tf_op jit(solution)/shard_map/gather_grams/pallas_call | solution.py:527
  26.6 5.6 %analyse.1 = f32[1,1,512,1024]{3,2,1,0:T(8,128)} custom-call(f32[1040,128]{1,0:T(8,128)} %get-tuple-element.8.packed, f32[8,1024]{1,0:T(8,128)} %get-tuple-element.9.state_mean, bf16[512,1024]{1,0:T(8,128)(2,1)} %get-tuple-element.10.spread), custom_call_target="tpu_custom_call" | custom-call | flops 1879048192 | bytes 3145728 | tf_op jit(solution)/shard_map/analyse/pallas_call | solution.py:572

commit v4 on v3

--- a/solution.py
+++ b/solution.py
@@ -438,7 +438,9 @@
     lax.fori_loop(0, chips - 1, drain, 0)
 
 
-def analyse_kernel(packed, state_mean, spread, out, anomaly_buf, out_buf, load, store):
+def analyse_kernel(
+    packed, state_mean, spread, out, anomaly_buf, out_buf, y, u, w, e, f, h, t, load, store
+):
     members = spread.shape[0]
     fetch = pltpu.make_async_copy(spread, anomaly_buf, load)
     fetch.start()
@@ -457,48 +459,52 @@
     drive = tail_row(0, lane_blocks)
     diagonal = tail_row(2, lane_blocks // 2)
     row, col = iota((half, half), 0), iota((half, half), 1)
+    on = row == col
     strict = jnp.where(row < col, field, 0.0)
     under = jnp.where(row > col, field, 0.0)
-    first = jnp.where(row <= col, field, 0.0) + strict.T
-    second = under + under.T + jnp.where(row == col, diagonal, 0.0)
-    gram = jnp.concatenate(
-        [jnp.concatenate([first, cross], axis=1), jnp.concatenate([cross.T, second], axis=1)], axis=0
-    )
-    one = (iota((members, members), 0) == iota((members, members), 1)).astype(F32)
-    system = (members - 1.0) * one + gram
-    scale = jnp.sqrt(jnp.sum(jnp.sum(system * system, axis=0, keepdims=True), axis=1, keepdims=True))
-    y = system / scale
-    yb = y.astype(BF16)
-    square = dot(yb, yb)
-    u = 1.5 * y - 0.5 * square
-    w = 0.25 * square - 1.5 * y
-    q = 2.25 * u + dot(u.astype(BF16), w.astype(BF16))
-    e2 = -0.75 * y - 0.5 * q
-    e2b = e2.astype(BF16)
-    f = 2.25 * y + dot(yb, e2b)
-    h = 4.5 * e2 + dot(e2b, e2b)
-    e3 = 1.5 * e2 - 0.5 * (5.0625 * f + dot(f.astype(BF16), h.astype(BF16)))
-    e3b = e3.astype(BF16)
+    first = strict + strict.T + jnp.where(on, field + (members - 1.0), 0.0)
+    second = under + under.T + jnp.where(on, diagonal + (members - 1.0), 0.0)
+    squares = first * first + second * second + 2.0 * cross * cross
+    square_sum = jnp.sum(jnp.sum(squares, axis=0, keepdims=True), axis=1, keepdims=True)
+    scale = jnp.sqrt(square_sum)
+    shrink = 1.0 / scale
+    upper_right = cross * shrink
+    y[:half, :half] = (first * shrink).astype(BF16)
+    y[half:, half:] = (second * shrink).astype(BF16)
+    y[:half, half:] = upper_right.astype(BF16)
+    y[half:, :half] = upper_right.T.astype(BF16)
+
+    bands = [slice(at * half, (at + 1) * half) for at in range(2)]
+    for band in bands:
+        own = y[band, :].astype(F32)
+        square = dot(y[band, :], y[...])
+        u[band, :] = (1.5 * own - 0.5 * square).astype(BF16)
+        w[band, :] = (0.25 * square - 1.5 * own).astype(BF16)
+    for band in bands:
+        product = dot(u[band, :], w[...])
+        e[band, :] = (
+            -0.75 * y[band, :].astype(F32) - 1.125 * u[band, :].astype(F32) - 0.5 * product
+        ).astype(BF16)
+    for band in bands:
+        f[band, :] = (2.25 * y[band, :].astype(F32) + dot(y[band, :], e[...])).astype(BF16)
+        h[band, :] = (4.5 * e[band, :].astype(F32) + dot(e[band, :], e[...])).astype(BF16)
+    for band in bands:
+        product = dot(f[band, :], h[...])
+        t[band, :] = (
+            1.5 * e[band, :].astype(F32) - 2.53125 * f[band, :].astype(F32) - 0.5 * product
+        ).astype(BF16)
 
     def times_root(vector):
         high = vector.astype(BF16)
         low = (vector - high.astype(F32)).astype(BF16)
         place = iota((16, members), 0)
         both = jnp.where(place == 0, high.astype(F32), jnp.where(place == 1, low.astype(F32), 0.0))
-        product = dot(both.astype(BF16), e3b)
+        product = dot(both.astype(BF16), t[...])
         return 3.375 * vector + product[0:1] + product[1:2]
 
-    mean_weight = times_root(times_root(drive)) / scale
-    transform = (jnp.sqrt((members - 1.0) / scale) * (3.375 * one + e3)).astype(BF16)
-
+    mean_weight = times_root(times_root(drive)) * shrink
+    gain = jnp.sqrt((members - 1.0) * shrink)
     fetch.wait()
-    anomaly = anomaly_buf[...]
-    high = mean_weight.astype(BF16)
-    low = (mean_weight - high.astype(F32)).astype(BF16)
-    place = iota((16, members), 0)
-    both = jnp.where(place == 0, high.astype(F32), jnp.where(place == 1, low.astype(F32), 0.0))
-    shift = dot(both.astype(BF16), anomaly)
-    centre = state_mean[0:1] + shift[0:1] + shift[1:2]
     part = members // STORES
     stores = [
         pltpu.make_async_copy(
@@ -507,7 +513,11 @@
         for at in range(STORES)
     ]
     for at, copy in enumerate(stores):
-        out_buf[at * part : (at + 1) * part, :] = dot(transform[at * part : (at + 1) * part], anomaly) + centre
+        band = slice(at * part, (at + 1) * part)
+        one = iota((part, members), 0) + at * part == iota((part, members), 1)
+        root = t[band, :].astype(F32) + jnp.where(one, 3.375, 0.0)
+        transform = (gain * root + mean_weight).astype(BF16)
+        out_buf[band, :] = dot(transform, anomaly_buf[...]) + state_mean[0:1]
         copy.start()
     for copy in stores:
         copy.wait()
@@ -577,6 +587,7 @@
         scratch_shapes=[
             pltpu.VMEM((members, cells), BF16),
             pltpu.VMEM((members, cells), F32),
+            *[pltpu.VMEM((members, members), BF16)] * 7,
             pltpu.SemaphoreType.DMA,
             pltpu.SemaphoreType.DMA((STORES,)),
         ],

time: 32.3 us -> 31.9 us (0.988)
    pallas_call x1, Pallas kernels: 5.55 us -> 5.2 us  [shards(): pl.pallas_call(analyse_kernel, out_shape=jax.ShapeDtypeStruct((1, 1, memb...]
where the time goes in v4:
time: 31.9 us; the launch traced here: 31.8 us
  Pallas kernels  31.8 us (100%)
    pallas_call x1, Pallas kernels, shards(): pl.pallas_call(functools.partial(gather_kernel, n_lat, n_lon), out_shape=...  26.6 us
    pallas_call x1, Pallas kernels, shards(): pl.pallas_call(analyse_kernel, out_shape=jax.ShapeDtypeStruct((1, 1, memb...  5.2 us

profile of v4, /device:TPU:0, one launch (start us, length us, event | category | flops | bytes accessed | tf_op | source)
XLA Modules:
  0.0 31.8 jit_solution(6540585155257342546)
XLA Ops:
  0.0 26.6 %gather_grams.1 = (f32[1040,128]{1,0:T(8,128)}, bf16[512,1024]{1,0:T(8,128)(2,1)}, f32[8,1024]{1,0:T(8,128)}) custom-call(bf16[1,1,512,1024]{3,2,1,0:T(8,128)(2,1)} %background.1, bf16[1,1,128,512]{3,2,1,0:T(8,128)(2,1)} %conv_pert.1, bf16[1,1,128]{2,1,0:T(2,128)(2,1)} %conv_misfit.1, s32[1,1,128]{2,1,0:T(1,128)} %conv_column.1, bf16[512,512]{1,0:T(8,128)(2,1)} %bitcast.2, ...), custom_call_target="tpu_custom_call" | custom-call | flops 2751463424 | bytes 1048576 | tf_op jit(solution)/shard_map/gather_grams/pallas_call | solution.py:537
  26.6 5.2 %analyse.1 = f32[1,1,512,1024]{3,2,1,0:T(8,128)} custom-call(f32[1040,128]{1,0:T(8,128)} %get-tuple-element.8.packed, f32[8,1024]{1,0:T(8,128)} %get-tuple-element.9.state_mean, bf16[512,1024]{1,0:T(8,128)(2,1)} %get-tuple-element.10.spread), custom_call_target="tpu_custom_call" | custom-call | flops 1879048192 | bytes 3145728 | tf_op jit(solution)/shard_map/analyse/pallas_call | solution.py:582

commit v5 on v4

--- a/solution.py
+++ b/solution.py
@@ -85,9 +85,11 @@
             device_id=(band, sibling), device_id_type=MESH,
         )
 
-    tile_copy = sat_copy(sat_pert, sat_buf.at[1], 0)
-    list_copy = sat_copy(sat_lists.at[0], sat_lists.at[1], 1)
-    tile_copy.start()
+    spans = [pl.ds(at * (rows // 2), rows // 2) for at in range(2)]
+    tile_copies = [sat_copy(sat_pert.at[span], sat_buf.at[1, span], at) for at, span in enumerate(spans)]
+    list_copy = sat_copy(sat_lists.at[0], sat_lists.at[1], 2)
+    for copy in tile_copies:
+        copy.start()
 
     for copy in loads[:6]:
         copy.wait()
@@ -149,22 +151,23 @@
     list_copy.start()
     to_side.start()
 
-    blank = jnp.zeros((conv_obs + EXTRA, members), BF16)
-
-    @pl.when(jnp.logical_not(has_north))
-    def _():
-        for group in range(3):
-            conv_buf[group, 0] = blank
-
-    @pl.when(jnp.logical_not(has_south))
-    def _():
-        for group in range(3):
-            conv_buf[group, 2] = blank
-
-    def flip_sat(side):
-        sat_flip[side] = sat_buf[side].T
+    def flip_sat(side, part, span):
+        lanes = slice(part * half, (part + 1) * half)
+        sat_flip[side, lanes, span] = sat_buf[side, span, lanes].T
 
     def relay():
+        blank = jnp.zeros((conv_obs + EXTRA, members), BF16)
+
+        @pl.when(jnp.logical_not(has_north))
+        def _():
+            for group in range(3):
+                conv_buf[group, 0] = blank
+
+        @pl.when(jnp.logical_not(has_south))
+        def _():
+            for group in range(3):
+                conv_buf[group, 2] = blank
+
         @pl.when(has_north)
         def _():
             to_south.wait_recv()
@@ -308,27 +311,35 @@
         line_copy(way, to_chip, part).start()
 
     loads[6].wait()
-    flip_sat(0)
+    for span in spans:
+        flip_sat(0, 0, span)
     for way in range(2):
         to_chip, wanted, _ = step_of(way, 0)
 
         @pl.when(wanted)
         def _():
-            for part in range(2):
-                add_sat(way, part, to_chip, 0)
+            add_sat(way, 0, to_chip, 0)
 
     list_copy.wait_recv()
-    tile_copy.wait_recv()
-    flip_sat(1)
+    for copy, span in zip(tile_copies, spans):
+        copy.wait_recv()
+        flip_sat(1, 0, span)
 
     def step_body(step, carry):
         for part in range(2):
+            if part == 1:
+                @pl.when(step == 0)
+                def _():
+                    for side in range(2):
+                        for span in spans:
+                            flip_sat(side, 1, span)
+
             for way in range(2):
                 to_chip, wanted, behind = step_of(way, step)
 
                 @pl.when(wanted)
                 def _():
-                    @pl.when(step > 0)
+                    @pl.when(jnp.logical_or(step > 0, part == 1))
                     def _():
                         add_sat(way, part, to_chip, 0)
 
@@ -399,7 +410,8 @@
         out[parts[part], :] = acc[0, parts[part], :]
 
     keep.wait()
-    tile_copy.wait_send()
+    for copy in tile_copies:
+        copy.wait_send()
     list_copy.wait_send()
     to_side.wait_send()
 
@@ -460,12 +472,16 @@
     diagonal = tail_row(2, lane_blocks // 2)
     row, col = iota((half, half), 0), iota((half, half), 1)
     on = row == col
-    strict = jnp.where(row < col, field, 0.0)
-    under = jnp.where(row > col, field, 0.0)
-    first = strict + strict.T + jnp.where(on, field + (members - 1.0), 0.0)
-    second = under + under.T + jnp.where(on, diagonal + (members - 1.0), 0.0)
-    squares = first * first + second * second + 2.0 * cross * cross
-    square_sum = jnp.sum(jnp.sum(squares, axis=0, keepdims=True), axis=1, keepdims=True)
+    turned = field.T
+    first = jnp.where(row < col, field, turned) + jnp.where(on, members - 1.0, 0.0)
+    second = jnp.where(on, diagonal + (members - 1.0), jnp.where(row > col, field, turned))
+    lone = diagonal + (members - 1.0)
+    apart = jnp.where(on, 0.0, field)
+    kept = field + (members - 1.0)
+    squares = 2.0 * (apart * apart + cross * cross) + jnp.where(on, kept * kept, 0.0)
+    square_sum = jnp.sum(
+        jnp.sum(squares, axis=0, keepdims=True) + lone * lone, axis=1, keepdims=True
+    )
     scale = jnp.sqrt(square_sum)
     shrink = 1.0 / scale
     upper_right = cross * shrink
@@ -488,21 +504,22 @@
     for band in bands:
         f[band, :] = (2.25 * y[band, :].astype(F32) + dot(y[band, :], e[...])).astype(BF16)
         h[band, :] = (4.5 * e[band, :].astype(F32) + dot(e[band, :], e[...])).astype(BF16)
+    def times(vector, matrix):
+        high = vector.astype(BF16)
+        low = (vector - high.astype(F32)).astype(BF16)
+        place = iota((16, members), 0)
+        both = jnp.where(place == 0, high.astype(F32), jnp.where(place == 1, low.astype(F32), 0.0))
+        product = dot(both.astype(BF16), matrix[...])
+        return product[0:1] + product[1:2]
+
+    drive_f = times(drive, f)
+    push = 3.375 * drive + 1.5 * times(drive, e) - 2.53125 * drive_f - 0.5 * times(drive_f, h)
     for band in bands:
         product = dot(f[band, :], h[...])
         t[band, :] = (
             1.5 * e[band, :].astype(F32) - 2.53125 * f[band, :].astype(F32) - 0.5 * product
         ).astype(BF16)
-
-    def times_root(vector):
-        high = vector.astype(BF16)
-        low = (vector - high.astype(F32)).astype(BF16)
-        place = iota((16, members), 0)
-        both = jnp.where(place == 0, high.astype(F32), jnp.where(place == 1, low.astype(F32), 0.0))
-        product = dot(both.astype(BF16), t[...])
-        return 3.375 * vector + product[0:1] + product[1:2]
-
-    mean_weight = times_root(times_root(drive)) * shrink
+    mean_weight = (3.375 * push + times(push, t)) * shrink
     gain = jnp.sqrt((members - 1.0) * shrink)
     fetch.wait()
     part = members // STORES
@@ -560,8 +577,8 @@
             pltpu.VMEM((2, chips, lanes_long, LANES), BF16),
             pltpu.VMEM((2, chips, lanes_long, LANES), BF16),
             pltpu.SemaphoreType.DMA((9,)),
-            pltpu.SemaphoreType.DMA((2,)),
-            pltpu.SemaphoreType.DMA((2,)),
+            pltpu.SemaphoreType.DMA((3,)),
+            pltpu.SemaphoreType.DMA((3,)),
             pltpu.SemaphoreType.DMA((8,)),
             pltpu.SemaphoreType.DMA((8,)),
             pltpu.SemaphoreType.DMA((2, chips, 2)),

time: 31.9 us -> 32.1 us (level)
  no operation moved by 1% of the time
where the time goes in v5:
time: 32.1 us; the launch traced here: 31.9 us
  Pallas kernels  31.9 us (99%)
    pallas_call x1, Pallas kernels, shards(): pl.pallas_call(functools.partial(gather_kernel, n_lat, n_lon), out_shape=...  26.7 us
    pallas_call x1, Pallas kernels, shards(): pl.pallas_call(analyse_kernel, out_shape=jax.ShapeDtypeStruct((1, 1, memb...  5.23 us

profile of v5, /device:TPU:0, one launch (start us, length us, event | category | flops | bytes accessed | tf_op | source)
XLA Modules:
  0.0 31.9 jit_solution(15855366670538537912)
XLA Ops:
  0.0 26.7 %gather_grams.1 = (f32[1040,128]{1,0:T(8,128)}, bf16[512,1024]{1,0:T(8,128)(2,1)}, f32[8,1024]{1,0:T(8,128)}) custom-call(bf16[1,1,512,1024]{3,2,1,0:T(8,128)(2,1)} %background.1, bf16[1,1,128,512]{3,2,1,0:T(8,128)(2,1)} %conv_pert.1, bf16[1,1,128]{2,1,0:T(2,128)(2,1)} %conv_misfit.1, s32[1,1,128]{2,1,0:T(1,128)} %conv_column.1, bf16[512,512]{1,0:T(8,128)(2,1)} %bitcast.2, ...), custom_call_target="tpu_custom_call" | custom-call | flops 2751463424 | bytes 1048576 | tf_op jit(solution)/shard_map/gather_grams/pallas_call | solution.py:554
  26.7 5.2 %analyse.1 = f32[1,1,512,1024]{3,2,1,0:T(8,128)} custom-call(f32[1040,128]{1,0:T(8,128)} %get-tuple-element.8.packed, f32[8,1024]{1,0:T(8,128)} %get-tuple-element.9.state_mean, bf16[512,1024]{1,0:T(8,128)(2,1)} %get-tuple-element.10.spread), custom_call_target="tpu_custom_call" | custom-call | flops 1879048192 | bytes 3145728 | tf_op jit(solution)/shard_map/analyse/pallas_call | solution.py:599

commit v6 on v5

--- a/solution.py
+++ b/solution.py
@@ -325,6 +325,21 @@
         copy.wait_recv()
         flip_sat(1, 0, span)
 
+    keep = pltpu.make_async_copy(anomaly_buf, anomaly, load.at[8])
+
+    own_step = jnp.where(jnp.logical_and(has_low, has_high), 0, chips - 2)
+
+    def own_terms():
+        for part in range(2):
+            for side in range(2):
+                add_sat(2, part, chip, side)
+        loads[7].wait()
+        ensemble = members_buf[...].astype(F32)
+        state_mean = jnp.mean(ensemble, axis=0, keepdims=True)
+        anomaly_buf[...] = (ensemble - state_mean).astype(BF16)
+        keep.start()
+        centre[...] = jnp.broadcast_to(state_mean, centre.shape)
+
     def step_body(step, carry):
         for part in range(2):
             if part == 1:
@@ -363,6 +378,10 @@
             def _():
                 relay()
 
+        @pl.when(step == own_step)
+        def _():
+            own_terms()
+
         return carry
 
     if chips == 2:
@@ -375,9 +394,7 @@
         conv_ready()
 
     for part in range(2):
-        for side in range(2):
-            add_sat(0, part, chip, side)
-        add_conv(0, part, block, (0, 1))
+        add_conv(2, part, block, (0, 1))
 
     @pl.when(outer)
     def _():
@@ -390,24 +407,16 @@
             far_north.wait_recv()
 
         for part in range(2):
-            add_conv(0, part, block, (2,))
-
-    loads[7].wait()
-    ensemble = members_buf[...].astype(F32)
-    state_mean = jnp.mean(ensemble, axis=0, keepdims=True)
-    anomaly_buf[...] = (ensemble - state_mean).astype(BF16)
-    keep = pltpu.make_async_copy(anomaly_buf, anomaly, load.at[8])
-    keep.start()
-    centre[...] = jnp.broadcast_to(state_mean, centre.shape)
+            add_conv(2, part, block, (2,))
 
     for part in range(2):
         for way, behind in enumerate((has_low, has_high)):
             @pl.when(behind)
             def _():
                 line_copy(way, chip, part).wait_recv()
-                acc[0, parts[part], :] += recv_buf[way, chip, parts[part], :].astype(F32)
-
-        out[parts[part], :] = acc[0, parts[part], :]
+                acc[2, parts[part], :] += recv_buf[way, chip, parts[part], :].astype(F32)
+
+        out[parts[part], :] = acc[2, parts[part], :]
 
     keep.wait()
     for copy in tile_copies:
@@ -573,7 +582,7 @@
             pltpu.VMEM((3, 3, conv_obs + EXTRA, members), BF16),
             pltpu.VMEM((2, members, rows), BF16),
             pltpu.VMEM((members, 6 * conv_obs), BF16),
-            pltpu.VMEM((2, lanes_long, LANES), F32),
+            pltpu.VMEM((3, lanes_long, LANES), F32),
             pltpu.VMEM((2, chips, lanes_long, LANES), BF16),
             pltpu.VMEM((2, chips, lanes_long, LANES), BF16),
             pltpu.SemaphoreType.DMA((9,)),

time: 32.1 us -> 32.1 us (level)
  no operation moved by 1% of the time
where the time goes in v6:
time: 32.1 us; the launch traced here: 31.9 us
  Pallas kernels  31.9 us (99%)
    pallas_call x1, Pallas kernels, shards(): pl.pallas_call(functools.partial(gather_kernel, n_lat, n_lon), out_shape=...  26.7 us
    pallas_call x1, Pallas kernels, shards(): pl.pallas_call(analyse_kernel, out_shape=jax.ShapeDtypeStruct((1, 1, memb...  5.22 us

profile of v6, /device:TPU:0, one launch (start us, length us, event | category | flops | bytes accessed | tf_op | source)
XLA Modules:
  0.0 31.9 jit_solution(6214849502839002900)
XLA Ops:
  0.0 26.7 %gather_grams.1 = (f32[1040,128]{1,0:T(8,128)}, bf16[512,1024]{1,0:T(8,128)(2,1)}, f32[8,1024]{1,0:T(8,128)}) custom-call(bf16[1,1,512,1024]{3,2,1,0:T(8,128)(2,1)} %background.1, bf16[1,1,128,512]{3,2,1,0:T(8,128)(2,1)} %conv_pert.1, bf16[1,1,128]{2,1,0:T(2,128)(2,1)} %conv_misfit.1, s32[1,1,128]{2,1,0:T(1,128)} %conv_column.1, bf16[512,512]{1,0:T(8,128)(2,1)} %bitcast.2, ...), custom_call_target="tpu_custom_call" | custom-call | flops 2751463424 | bytes 1048576 | tf_op jit(solution)/shard_map/gather_grams/pallas_call | solution.py:563
  26.7 5.2 %analyse.1 = f32[1,1,512,1024]{3,2,1,0:T(8,128)} custom-call(f32[1040,128]{1,0:T(8,128)} %get-tuple-element.8.packed, f32[8,1024]{1,0:T(8,128)} %get-tuple-element.9.state_mean, bf16[512,1024]{1,0:T(8,128)(2,1)} %get-tuple-element.10.spread), custom_call_target="tpu_custom_call" | custom-call | flops 1879048192 | bytes 3145728 | tf_op jit(solution)/shard_map/analyse/pallas_call | solution.py:608

commit v7 on v6

--- a/solution.py
+++ b/solution.py
@@ -13,7 +13,7 @@
 BF16 = jnp.bfloat16
 EXTRA = 16
 LANES = 128
-STORES = 4
+STORES = 2
 
 
 def dot(left, right):
@@ -373,14 +373,14 @@
                 def _():
                     finish(way, to_chip, behind, part)
 
+        @pl.when(step == own_step)
+        def _():
+            own_terms()
+
         if chips > 2:
-            @pl.when(step == 0)
+            @pl.when(step == chips - 3)
             def _():
                 relay()
-
-        @pl.when(step == own_step)
-        def _():
-            own_terms()
 
         return carry
 
@@ -499,7 +499,7 @@
     y[:half, half:] = upper_right.astype(BF16)
     y[half:, :half] = upper_right.T.astype(BF16)
 
-    bands = [slice(at * half, (at + 1) * half) for at in range(2)]
+    bands = [slice(0, members)]
     for band in bands:
         own = y[band, :].astype(F32)
         square = dot(y[band, :], y[...])

time: 32.1 us -> 32.2 us (level)
  no operation moved by 1% of the time
where the time goes in v7:
time: 32.2 us; the launch traced here: 32.1 us
  Pallas kernels  32.1 us (100%)
    pallas_call x1, Pallas kernels, shards(): pl.pallas_call(functools.partial(gather_kernel, n_lat, n_lon), out_shape=...  26.7 us
    pallas_call x1, Pallas kernels, shards(): pl.pallas_call(analyse_kernel, out_shape=jax.ShapeDtypeStruct((1, 1, memb...  5.35 us

profile of v7, /device:TPU:0, one launch (start us, length us, event | category | flops | bytes accessed | tf_op | source)
XLA Modules:
  0.0 32.1 jit_solution(3594375240976792479)
XLA Ops:
  0.0 26.7 %gather_grams.1 = (f32[1040,128]{1,0:T(8,128)}, bf16[512,1024]{1,0:T(8,128)(2,1)}, f32[8,1024]{1,0:T(8,128)}) custom-call(bf16[1,1,512,1024]{3,2,1,0:T(8,128)(2,1)} %background.1, bf16[1,1,128,512]{3,2,1,0:T(8,128)(2,1)} %conv_pert.1, bf16[1,1,128]{2,1,0:T(2,128)(2,1)} %conv_misfit.1, s32[1,1,128]{2,1,0:T(1,128)} %conv_column.1, bf16[512,512]{1,0:T(8,128)(2,1)} %bitcast.2, ...), custom_call_target="tpu_custom_call" | custom-call | flops 2751463424 | bytes 1048576 | tf_op jit(solution)/shard_map/gather_grams/pallas_call | solution.py:563
  26.7 5.3 %analyse.1 = f32[1,1,512,1024]{3,2,1,0:T(8,128)} custom-call(f32[1040,128]{1,0:T(8,128)} %get-tuple-element.8.packed, f32[8,1024]{1,0:T(8,128)} %get-tuple-element.9.state_mean, bf16[512,1024]{1,0:T(8,128)(2,1)} %get-tuple-element.10.spread), custom_call_target="tpu_custom_call" | custom-call | flops 1879048192 | bytes 3145728 | tf_op jit(solution)/shard_map/analyse/pallas_call | solution.py:608

commit v8 on v7

--- a/solution.py
+++ b/solution.py
@@ -13,7 +13,7 @@
 BF16 = jnp.bfloat16
 EXTRA = 16
 LANES = 128
-STORES = 2
+STORES = 4
 
 
 def dot(left, right):
@@ -499,7 +499,7 @@
     y[:half, half:] = upper_right.astype(BF16)
     y[half:, :half] = upper_right.T.astype(BF16)
 
-    bands = [slice(0, members)]
+    bands = [slice(at * half, (at + 1) * half) for at in range(2)]
     for band in bands:
         own = y[band, :].astype(F32)
         square = dot(y[band, :], y[...])
@@ -521,13 +521,12 @@
         product = dot(both.astype(BF16), matrix[...])
         return product[0:1] + product[1:2]
 
-    drive_f = times(drive, f)
-    push = 3.375 * drive + 1.5 * times(drive, e) - 2.53125 * drive_f - 0.5 * times(drive_f, h)
     for band in bands:
         product = dot(f[band, :], h[...])
         t[band, :] = (
             1.5 * e[band, :].astype(F32) - 2.53125 * f[band, :].astype(F32) - 0.5 * product
         ).astype(BF16)
+    push = 3.375 * drive + times(drive, t)
     mean_weight = (3.375 * push + times(push, t)) * shrink
     gain = jnp.sqrt((members - 1.0) * shrink)
     fetch.wait()

time: 32.2 us -> 32 us (level)
  no operation moved by 1% of the time
where the time goes in v8:
time: 32 us; the launch traced here: 31.8 us
  Pallas kernels  31.8 us (99%)
    pallas_call x1, Pallas kernels, shards(): pl.pallas_call(functools.partial(gather_kernel, n_lat, n_lon), out_shape=...  26.7 us
    pallas_call x1, Pallas kernels, shards(): pl.pallas_call(analyse_kernel, out_shape=jax.ShapeDtypeStruct((1, 1, memb...  5.12 us

profile of v8, /device:TPU:0, one launch (start us, length us, event | category | flops | bytes accessed | tf_op | source)
XLA Modules:
  0.0 31.8 jit_solution(8382248642865047350)
XLA Ops:
  0.0 26.7 %gather_grams.1 = (f32[1040,128]{1,0:T(8,128)}, bf16[512,1024]{1,0:T(8,128)(2,1)}, f32[8,1024]{1,0:T(8,128)}) custom-call(bf16[1,1,512,1024]{3,2,1,0:T(8,128)(2,1)} %background.1, bf16[1,1,128,512]{3,2,1,0:T(8,128)(2,1)} %conv_pert.1, bf16[1,1,128]{2,1,0:T(2,128)(2,1)} %conv_misfit.1, s32[1,1,128]{2,1,0:T(1,128)} %conv_column.1, bf16[512,512]{1,0:T(8,128)(2,1)} %bitcast.2, ...), custom_call_target="tpu_custom_call" | custom-call | flops 2751463424 | bytes 1048576 | tf_op jit(solution)/shard_map/gather_grams/pallas_call | solution.py:562
  26.7 5.1 %analyse.1 = f32[1,1,512,1024]{3,2,1,0:T(8,128)} custom-call(f32[1040,128]{1,0:T(8,128)} %get-tuple-element.8.packed, f32[8,1024]{1,0:T(8,128)} %get-tuple-element.9.state_mean, bf16[512,1024]{1,0:T(8,128)(2,1)} %get-tuple-element.10.spread), custom_call_target="tpu_custom_call" | custom-call | flops 1879048192 | bytes 3145728 | tf_op jit(solution)/shard_map/analyse/pallas_call | solution.py:607
